TPU v7x, 32 devices: a whole 2x2x4 slice. The times are simulated.
32 devices in a mesh: patch: 16 (over z, y, x), shard: 2 (over core).
Axes of the slice: x: 2, y: 2, z: 4, core: 2. Of those that a mesh axis runs over, the one named last changes fastest.
Arguments:
- node_latent: bfloat16 [4096, 512], P(('patch', 'shard')), may hold values from -6 to 6
- edge_latent: bfloat16 [32768, 512], P(('patch', 'shard')), may hold values from -6 to 6
- senders: int32 [32768], P(('patch', 'shard')), may hold values from 0 to 383
- receivers: int32 [32768], P(('patch', 'shard')), may hold values from 0 to 255
- halo_list: int32 [16, 128], P('patch'), may hold values from 0 to 255
- w_edge_first: bfloat16 [1536, 512], replicated, may hold values from -0.15625 to 0.15625
- w_edge_second: bfloat16 [512, 512], replicated, may hold values from -0.25 to 0.25
- w_node_first: bfloat16 [1024, 512], replicated, may hold values from -0.1875 to 0.1875
- w_node_second: bfloat16 [512, 512], replicated, may hold values from -0.25 to 0.25
- grad_node_new: bfloat16 [4096, 512], P(('patch', 'shard')), may hold values from -6 to 6
- grad_edge_new: bfloat16 [32768, 512], P(('patch', 'shard')), may hold values from -6 to 6
Outputs:
- grad_node_latent: bfloat16 [4096, 512], P(('patch', 'shard'))
- grad_edge_latent: bfloat16 [32768, 512], P(('patch', 'shard'))
- grad_edge_first: float32 [1536, 512], P(None, 'patch')
- grad_edge_second: float32 [512, 512], P(None, 'patch')
- grad_node_first: float32 [1024, 512], P(None, 'patch')
- grad_node_second: float32 [512, 512], P(None, 'patch')
All inputs are finite; a program needn't handle non-finite values.
Results may differ from a plain program's by a relative error of at most 0.03.
Values may be sent and summed in bfloat16 or wider, within the bound.
A program may use at most 128 MiB of HBM per device.

v0:
```python
import jax
import jax.numpy as jnp
from jax import lax
from jax.sharding import PartitionSpec as P

epsilon = 1e-05


def padded(block, sides, width):
    for axis, dim in sides:
        count = lax.axis_size(axis)
        forward = [(i, i + 1) for i in range(count - 1)]
        forward.append((count - 1, 0))
        backward = [(target, source) for source, target in forward]
        low = lax.ppermute(
            lax.slice_in_dim(block, block.shape[dim] - width, None, axis=dim), axis, forward
        )
        high = lax.ppermute(lax.slice_in_dim(block, 0, width, axis=dim), axis, backward)
        block = jnp.concatenate([low, block, high], axis=dim)
    return block


def swish_slope(values):
    sig = jax.nn.sigmoid(values)
    return sig * (1.0 + values * (1.0 - sig))


def contract_rows(left, right):
    return lax.dot_general(
        left, right, (((0,), (0,)), ((), ())), preferred_element_type=jnp.float32
    )


def times_transpose(left, right):
    return lax.dot_general(
        left, right, (((1,), (1,)), ((), ())), preferred_element_type=jnp.float32
    )


def mlp_forward(joined, w_first, w_second):
    pre_act = jnp.dot(joined, w_first, preferred_element_type=jnp.float32)
    activated = (pre_act * jax.nn.sigmoid(pre_act)).astype(jnp.bfloat16)
    output = jnp.dot(activated, w_second, preferred_element_type=jnp.float32)
    center = output - jnp.mean(output, axis=-1, keepdims=True)
    inv_scale = lax.rsqrt(jnp.mean(center * center, axis=-1, keepdims=True) + epsilon)
    return (pre_act, activated, center * inv_scale, inv_scale)


def mlp_backward(joined, w_first, w_second, pre_act, activated, normed, inv_scale, cotangent):
    d_out = inv_scale * (
        cotangent
        - jnp.mean(cotangent, axis=-1, keepdims=True)
        - normed * jnp.mean(cotangent * normed, axis=-1, keepdims=True)
    )
    d_out = d_out.astype(jnp.bfloat16)
    d_act = times_transpose(d_out, w_second)
    d_pre = (d_act * swish_slope(pre_act)).astype(jnp.bfloat16)
    grad_second = contract_rows(activated, d_out)
    grad_first = contract_rows(joined, d_pre)
    d_joined = times_transpose(d_pre, w_first)
    return (d_joined, grad_first, grad_second)


def body(
    node_latent,
    edge_latent,
    senders,
    receivers,
    halo_list,
    w_edge_first,
    w_edge_second,
    w_node_first,
    w_node_second,
    grad_node_new,
    grad_edge_new,
):
    shards = lax.axis_size("shard")
    node_rows = node_latent.shape[0]
    width = node_latent.shape[1]
    patch_rows = node_rows * shards
    send_lists = halo_list[0]
    halo_width = send_lists.shape[0] // 2
    gathered = lax.all_gather(node_latent, "shard", axis=0, tiled=True)
    outgoing = jnp.take(gathered, send_lists, axis=0)
    widened = padded(outgoing, (("patch", 0),), halo_width)
    from_prev = widened[:halo_width]
    from_next = widened[halo_width * 3 :]
    extended = jnp.concatenate([from_prev, gathered, from_next], axis=0)
    joined = jnp.concatenate(
        [edge_latent, jnp.take(extended, senders, axis=0), jnp.take(gathered, receivers, axis=0)],
        axis=1,
    )
    pre_act, activated, normed, inv_scale = mlp_forward(joined, w_edge_first, w_edge_second)
    edge_new = (edge_latent.astype(jnp.float32) + normed).astype(jnp.bfloat16)
    partial_value = jax.ops.segment_sum(
        edge_new.astype(jnp.float32), receivers, num_segments=patch_rows
    )
    aggregate = lax.psum_scatter(
        partial_value.astype(jnp.bfloat16), "shard", scatter_dimension=0, tiled=True
    )
    node_joined = jnp.concatenate([node_latent, aggregate], axis=1)
    n_pre, n_act, n_normed, n_inv = mlp_forward(node_joined, w_node_first, w_node_second)
    node_grad = grad_node_new.astype(jnp.float32)
    d_node, g_node_first, g_node_second = mlp_backward(
        node_joined, w_node_first, w_node_second, n_pre, n_act, n_normed, n_inv, node_grad
    )
    d_aggregate = d_node[:, width:]
    spread = lax.all_gather(d_aggregate.astype(jnp.bfloat16), "shard", axis=0, tiled=True).astype(
        d_aggregate.dtype
    )
    edge_grad = grad_edge_new.astype(jnp.float32) + jnp.take(spread, receivers, axis=0)
    d_edge, g_edge_first, g_edge_second = mlp_backward(
        joined, w_edge_first, w_edge_second, pre_act, activated, normed, inv_scale, edge_grad
    )
    grad_edge_latent = (edge_grad + d_edge[:, :width]).astype(jnp.bfloat16)
    sender_part = jax.ops.segment_sum(
        d_edge[:, width : 2 * width], senders, num_segments=patch_rows + 2 * halo_width
    )
    receiver_part = jax.ops.segment_sum(d_edge[:, 2 * width :], receivers, num_segments=patch_rows)
    back_part = jnp.concatenate(
        [sender_part[:halo_width], sender_part[halo_width + patch_rows :]], axis=0
    )
    returned = padded(back_part.astype(jnp.bfloat16), (("patch", 0),), halo_width).astype(
        back_part.dtype
    )
    own_rows = sender_part[halo_width : halo_width + patch_rows] + receiver_part
    own_rows = own_rows.at[send_lists[:halo_width]].add(returned[:halo_width])
    own_rows = own_rows.at[send_lists[halo_width:]].add(returned[halo_width * 3 :])
    node_total = lax.psum_scatter(
        own_rows.astype(jnp.bfloat16), "shard", scatter_dimension=0, tiled=True
    ).astype(jnp.float32)
    grad_node_latent = (node_total + node_grad + d_node[:, :width]).astype(jnp.bfloat16)
    summed = lax.psum(
        (g_edge_first, g_edge_second, g_node_first, g_node_second), ("patch", "shard")
    )
    patches = lax.axis_size("patch")
    patch_index = lax.axis_index("patch")
    sliced = tuple(
        (
            lax.dynamic_slice_in_dim(
                matrix, patch_index * (matrix.shape[1] // patches), matrix.shape[1] // patches, 1
            )
            for matrix in summed
        )
    )
    return (grad_node_latent, grad_edge_latent, sliced[0], sliced[1], sliced[2], sliced[3])


def solution(mesh):
    in_specs = (
        P(("patch", "shard"), None),
        P(("patch", "shard"), None),
        P(("patch", "shard")),
        P(("patch", "shard")),
        P("patch", None),
        P(),
        P(),
        P(),
        P(),
        P(("patch", "shard"), None),
        P(("patch", "shard"), None),
    )
    out_specs = (
        P(("patch", "shard"), None),
        P(("patch", "shard"), None),
        P(None, "patch"),
        P(None, "patch"),
        P(None, "patch"),
        P(None, "patch"),
    )
    return jax.shard_map(body, mesh=mesh, in_specs=in_specs, out_specs=out_specs, check_vma=False)
```

profile of v0, /device:TPU:1, one launch (start us, length us, event | category | flops | bytes accessed | tf_op | source)
XLA Modules:
  0.0 329.6 jit_solution(7242766363321461721)
XLA Ops:
  7.2 0.8 fusion.31
  8.0 0.7 compare_and_fusion.2
  8.7 2.2 all_gather.6
  10.9 0.7 pad_clamp_fusion
  11.6 0.8 gather_fusion
  12.5 6.4 %collective-permute-start.1 = (bf16[64,512]{1,0:T(8,128)(2,1)S(1)}, bf16[64,512]{1,0:T(8,128)(2,1)S(1)}, u32[]{:S(2)}, u32[]{:S(2)}) collective-permute-start(bf16[64,512]{1,0:T(8,128)(2,1)S(1)} %get-tuple-element.29), channel_id=1, source_target_pairs={{2,0},{4,2},{6,4},{8,6},{10,8},{12,10},{14,12},{16,14},{18,16},{20... | collective-permute-start | bytes 196616 | tf_op jit(solution)/shard_map/ppermute | solution.py:18
  18.9 5.1 %gather_fusion.2 = bf16[1024,512]{1,0:T(8,128)(2,1)} fusion(bf16[256,512]{1,0:T(8,128)(2,1)S(1)} %all_gather.6, s32[1024]{0:T(1024)S(1)} %get-tuple-element.39), kind=kCustom, calls=%fused_computation.2 | custom fusion | bytes 2101248 | tf_op jit(solution)/shard_map/jit(_take)/gather | solution.py:90
  24.0 2.3 copy.26
  26.3 2.3 broadcast_select_fusion
  28.6 2.3 copy.27
  30.9 5.0 %gather_fusion.1 = bf16[1024,512]{1,0:T(8,128)(2,1)} fusion(bf16[384,512]{1,0:T(8,128)(2,1)S(1)} %pad_maximum_fusion.3, s32[1024]{0:T(1024)S(1)} %fusion.29), kind=kCustom, calls=%fused_computation.1 | custom fusion | bytes 2101248 | tf_op jit(solution)/shard_map/jit(_take)/gather | solution.py:90
  35.9 2.4 copy.25
  38.3 1.4 broadcast_select_fusion.1
  39.8 3.3 multiply_convert_fusion.2
  43.1 0.8 fusion.43
  43.9 0.3 multiply_reduce_fusion.1
  44.2 1.0 copy-done.1
  45.2 1.7 fusion.7
  46.9 2.9 copy.30
  49.8 7.4 %scatter_custom_fusion = f32[256,512]{1,0:T(8,128)S(1)} fusion(s32[1024]{0:T(1024)S(1)} %copy-done.22, f32[1024,512]{1,0:T(8,128)} %copy.30, f32[]{:T(128)} %constant.52.clone.1), kind=kCustom, calls=%fused_computation.47 | custom fusion | flops 524288 | bytes 524800 | tf_op jit(solution)/shard_map/scatter-add | solution.py:95
  57.3 0.7 convert_element_type.61
  58.1 1.5 copy.28
  59.6 0.6 fusion.33
  60.2 7.3 %reduce-scatter.3.cloned.1.call-done = bf16[128,512]{1,0:T(8,128)(2,1)} async-done(((bf16[256,512]{1,0:T(8,128)(2,1)}), bf16[128,512]{1,0:T(8,128)(2,1)}) %reduce-scatter.3.cloned.1.call-update) | async-done | bytes 131088 | tf_op jit(solution)/shard_map/reduce_scatter | solution.py:98
  67.6 0.9 constant_dynamic-update-slice_fusion
  68.5 1.6 fusion.45
  70.1 1.5 fusion.44
  72.1 0.3 copy-done.6
  72.3 1.4 fusion.6
  73.7 0.5 fusion.46
  74.4 0.8 copy-done.9
  75.2 2.2 all_gather.7
  77.4 4.9 %gather_fusion.3 = f32[1024,512]{1,0:T(8,128)} fusion(f32[256,512]{1,0:T(8,128)S(1)} %convert_element_type.66, s32[1024]{0:T(1024)S(1)} %get-tuple-element.39), kind=kCustom, calls=%fused_computation.3 | custom fusion | bytes 4198400 | tf_op jit(solution)/shard_map/jit(_take)/gather | solution.py:111
  82.3 2.9 copy.31
  85.2 3.0 fusion.38
  88.2 0.4 copy-done.3
  88.7 0.8 multiply_convert_fusion.1
  89.4 0.5 copy-done.15
  89.9 1.7 fusion.49
  91.8 1.2 multiply_convert_fusion
  93.1 1.0 copy-done.33
  94.1 4.5 %fusion.47 = f32[1024,1536]{1,0:T(8,128)} fusion(bf16[1024,512]{1,0:T(8,128)(2,1)S(1)} %multiply_convert_fusion, bf16[1536,512]{1,0:T(8,128)(2,1)S(1)} %copy-done), kind=kOutput, calls=%fused_computation.105 | convolution fusion | flops 1610612736 | bytes 8912896 | tf_op jit(solution)/shard_map/dot_general | solution.py:35
  98.5 7.6 %scatter_custom_fusion.1 = f32[384,512]{1,0:T(8,128)S(1)} fusion(s32[1024]{0:T(1024)} %param.13, f32[1024,1536]{1,0:T(8,128)} %fusion.47, f32[]{:T(128)} %constant.52.clone.1), kind=kCustom, calls=%fused_computation.12 | custom fusion | flops 524288 | bytes 2884096 | tf_op jit(solution)/shard_map/scatter-add | solution.py:116
  106.2 0.7 fusion.41
  106.8 5.2 %collective-permute-start.3 = (bf16[64,512]{1,0:T(8,128)(2,1)}, bf16[64,512]{1,0:T(8,128)(2,1)}, u32[]{:S(2)}, u32[]{:S(2)}) collective-permute-start(bf16[64,512]{1,0:T(8,128)(2,1)} %get-tuple-element.27), channel_id=1, source_target_pairs={{2,0},{4,2},{6,4},{8,6},{10,8},{12,10},{14,12},{16,14},{18,16},{20... | collective-permute-start | bytes 196616 | tf_op jit(solution)/shard_map/ppermute | solution.py:18
  112.1 2.8 fusion.48
  114.9 0.9 slice.81
  115.7 9.2 %scatter_custom_fusion.2 = f32[256,512]{1,0:T(8,128)} fusion(f32[256,512]{1,0:T(8,128)} %slice.81, s32[1024]{0:T(1024)} %param.14, f32[1024,1536]{1,0:T(8,128)} %fusion.47), kind=kCustom, calls=%fused_computation.10 | custom fusion | flops 524288 | bytes 2621440 | tf_op jit(solution)/shard_map/scatter-add | solution.py:119
  125.0 3.1 scatter_custom_fusion.3
  128.1 3.1 scatter_custom_fusion.4
  131.2 1.8 convert_element_type.70
  133.0 0.3 all-reduce.3.cloned.1.call-start
  133.3 1.5 fusion.36
  134.8 5.7 %fusion.4 = f32[1536,512]{0,1:T(8,128)} fusion(bf16[1024,512]{1,0:T(8,128)(2,1)} %copy-done.33, bf16[1024,512]{0,1:T(8,128)(2,1)} %broadcast_select_fusion, bf16[1024,512]{0,1:T(8,128)(2,1)} %copy-done.13, bf16[1024,512]{0,1:T(8,128)(2,1)} %copy.27), kind=kOutput, calls=%fused_computation.24 | convolution fusion | flops 1620049920 | bytes 7340032 | tf_op jit(solution)/shard_map/dot_general | solution.py:29
  140.5 3.1 slice.86
  143.6 2.9 copy.34
  146.5 3.8 %add_convert_fusion = bf16[1024,512]{0,1:T(8,128)(2,1)} fusion(f32[1024,512]{0,1:T(8,128)} %copy.34, f32[1024,512]{0,1:T(8,128)} %copy.31, pred[1024]{0:T(1024)(128)(4,1)S(1)} %compare_and_fusion, bf16[1024,512]{0,1:T(8,128)(2,1)S(1)} %copy.28), kind=kLoop, calls=%fused_computation.14 | loop fusion | flops 2621440 | bytes 6292480 | tf_op jit(solution)/shard_map/convert_element_type | solution.py:115
  150.4 2.3 copy.33
  152.7 1.6 fusion.14
  154.3 162.6 %all-reduce.3.cloned.1.call-done = (f32[1536,512]{0,1:T(8,128)}, f32[512,512]{0,1:T(8,128)}, f32[1024,512]{0,1:T(8,128)}, f32[512,512]{0,1:T(8,128)}) async-done(((f32[1536,512]{0,1:T(8,128)}, f32[512,512]{0,1:T(8,128)}, f32[1024,512]{0,1:T(8,128)}, f32[512,512]{0,1:T(8,128)}), (f32[1536,512]{0,1:T(8,128)}, f32[512,512]{0,1:T(8,128)}, f32[1024,512]{0,1:T(8,128)}, ...) | async-done | bytes 7340048 | tf_op jit(solution)/shard_map/psum | solution.py:133
  316.9 1.6 constant_dynamic-slice_fusion.3
  318.6 1.5 constant_dynamic-slice_fusion.2
  320.0 1.6 constant_dynamic-slice_fusion.1
  321.6 1.5 constant_dynamic-slice_fusion
  (96 shorter events, 1.4 us)
Async XLA Ops:
  7.2 32.5 %copy-start = (bf16[1536,512]{1,0:T(8,128)(2,1)S(1)}, bf16[1536,512]{1,0:T(8,128)(2,1)}, u32[]{:S(2)}) copy-start(bf16[1536,512]{1,0:T(8,128)(2,1)} %param.16) | copy-start | bytes 4718596
  7.2 11.7 %copy-start.22 = (s32[1024]{0:T(1024)S(1)}, s32[1024]{0:T(1024)}, u32[]{:S(2)}) copy-start(s32[1024]{0:T(1024)} %param.14) | copy-start | bytes 12292
  7.2 60.4 %reduce-scatter.3.cloned.1.call-start = ((), (), s32[]{:S(2)}) async-start(), calls=%async_computation.2 | async-start | bytes 393216 | tf_op jit(solution)/shard_map/reduce_scatter | solution.py:98
  12.5 18.3 %collective-permute-start.1 = (bf16[64,512]{1,0:T(8,128)(2,1)S(1)}, bf16[64,512]{1,0:T(8,128)(2,1)S(1)}, u32[]{:S(2)}, u32[]{:S(2)}) collective-permute-start(bf16[64,512]{1,0:T(8,128)(2,1)S(1)} %get-tuple-element.29), channel_id=1, source_target_pairs={{2,0},{4,2},{6,4},{8,6},{10,8},{12,10},{14,12},{16,14},{18,16},{20... | collective-permute-start | bytes 196616 | tf_op jit(solution)/shard_map/ppermute | solution.py:18
  18.9 11.9 %collective-permute-start = (bf16[64,512]{1,0:T(8,128)(2,1)S(1)}, bf16[64,512]{1,0:T(8,128)(2,1)S(1)}, u32[]{:S(2)}, u32[]{:S(2)}) collective-permute-start(bf16[64,512]{1,0:T(8,128)(2,1)S(1)} %get-tuple-element.28), channel_id=1, source_target_pairs={{0,2},{2,4},{4,6},{6,8},{8,10},{10,12},{12,14},{14,16},{16,18},{18... | collective-permute-start | bytes 196616 | tf_op jit(solution)/shard_map/ppermute | solution.py:15
  24.0 2.3 copy-start.23
  35.9 3.8 %copy-start.4 = (bf16[1024,512]{0,1:T(8,128)(2,1)S(1)}, bf16[1024,512]{0,1:T(8,128)(2,1)}, u32[]{:S(2)}) copy-start(bf16[1024,512]{0,1:T(8,128)(2,1)} %copy.27) | copy-start | bytes 3145732
  38.3 1.5 copy-start.12
  39.8 3.3 copy-start.13
  39.8 3.3 copy-start.19
  43.1 1.1 copy-start.14
  43.9 1.3 copy-start.1
  49.8 9.7 %copy-start.18 = (bf16[128,512]{1,0:T(8,128)(2,1)S(1)}, bf16[128,512]{1,0:T(8,128)(2,1)}, u32[]{:S(2)}) copy-start(bf16[128,512]{1,0:T(8,128)(2,1)} %param.11) | copy-start | bytes 393220
  49.8 9.8 %copy-start.28 = (s32[1,128]{1,0:T(1,128)S(1)}, s32[1,128]{1,0:T(1,128)}, u32[]{:S(2)}) copy-start(s32[1,128]{1,0:T(1,128)} %param.15) | copy-start | bytes 1540
  58.0 94.7 %reduce-scatter.5.cloned.1.call-start = ((), (), s32[]{:S(2)}) async-start(), calls=%async_computation.3 | async-start | bytes 393216 | tf_op jit(solution)/shard_map/reduce_scatter | solution.py:129
  59.6 12.2 %copy-start.11 = (bf16[128,512]{1,0:T(8,128)(2,1)S(1)}, bf16[128,512]{1,0:T(8,128)(2,1)}, u32[]{:S(2)}) copy-start(bf16[128,512]{1,0:T(8,128)(2,1)} %param.20) | copy-start | bytes 393220
  68.5 5.2 %copy-start.8 = (bf16[128,1024]{1,0:T(8,128)(2,1)}, bf16[128,1024]{1,0:T(8,128)(2,1)S(1)}, u32[]{:S(2)}) copy-start(bf16[128,1024]{1,0:T(8,128)(2,1)S(1)} %constant_dynamic-update-slice_fusion) | copy-start | bytes 786436
  70.1 3.6 %copy-start.16 = (f32[128,512]{1,0:T(8,128)}, f32[128,512]{1,0:T(8,128)S(1)}, u32[]{:S(2)}) copy-start(f32[128,512]{1,0:T(8,128)S(1)} %fusion.45) | copy-start | bytes 786436
  70.1 3.6 %copy-start.5 = (bf16[1024,512]{1,0:T(8,128)(2,1)S(1)}, bf16[1024,512]{1,0:T(8,128)(2,1)}, u32[]{:S(2)}) copy-start(bf16[1024,512]{1,0:T(8,128)(2,1)} %param.18) | copy-start | bytes 3145732
  71.6 0.7 copy-start.6
  71.6 2.6 copy-start.24
  71.8 2.4 copy-start.26
  72.1 2.2 copy-start.29
  72.3 1.9 copy-start.31
  73.7 0.7 copy-start.21
  74.4 0.8 copy-start.9
  85.2 3.0 copy-start.2
  85.2 3.5 %copy-start.3 = (f32[1024,512]{0,1:T(8,128)S(1)}, f32[1024,512]{0,1:T(8,128)}, u32[]{:S(2)}) copy-start(f32[1024,512]{0,1:T(8,128)} %copy.31) | copy-start | bytes 6291460
  88.7 1.2 copy-start.15
  89.9 1.7 copy-start.20
  89.9 1.9 copy-start.34
  93.1 1.0 copy-start.33
  106.8 18.1 %collective-permute-start.3 = (bf16[64,512]{1,0:T(8,128)(2,1)}, bf16[64,512]{1,0:T(8,128)(2,1)}, u32[]{:S(2)}, u32[]{:S(2)}) collective-permute-start(bf16[64,512]{1,0:T(8,128)(2,1)} %get-tuple-element.27), channel_id=1, source_target_pairs={{2,0},{4,2},{6,4},{8,6},{10,8},{12,10},{14,12},{16,14},{18,16},{20... | collective-permute-start | bytes 196616 | tf_op jit(solution)/shard_map/ppermute | solution.py:18
  112.1 12.9 %collective-permute-start.2 = (bf16[64,512]{1,0:T(8,128)(2,1)}, bf16[64,512]{1,0:T(8,128)(2,1)}, u32[]{:S(2)}, u32[]{:S(2)}) collective-permute-start(bf16[64,512]{1,0:T(8,128)(2,1)} %get-tuple-element.26), channel_id=1, source_target_pairs={{0,2},{2,4},{4,6},{6,8},{8,10},{10,12},{12,14},{14,16},{16,18},{18... | collective-permute-start | bytes 196616 | tf_op jit(solution)/shard_map/ppermute | solution.py:15
  115.7 17.6 %copy-start.7 = (f32[128,512]{1,0:T(8,128)S(1)}, f32[128,512]{1,0:T(8,128)}, u32[]{:S(2)}) copy-start(f32[128,512]{1,0:T(8,128)} %copy-done.6) | copy-start | bytes 786436
  115.7 17.6 %copy-start.17 = (f32[128,512]{1,0:T(8,128)S(1)}, f32[128,512]{1,0:T(8,128)}, u32[]{:S(2)}) copy-start(f32[128,512]{1,0:T(8,128)} %copy-done.16) | copy-start | bytes 786436
  115.7 17.6 %copy-start.25 = (f32[128]{0:T(128)S(1)}, f32[128]{0:T(128)}, u32[]{:S(2)}) copy-start(f32[128]{0:T(128)} %copy-done.24) | copy-start | bytes 1540
  115.7 17.6 %copy-start.27 = (f32[128]{0:T(128)S(1)}, f32[128]{0:T(128)}, u32[]{:S(2)}) copy-start(f32[128]{0:T(128)} %copy-done.26) | copy-start | bytes 1540
  115.7 17.6 %copy-start.30 = (f32[128]{0:T(128)S(1)}, f32[128]{0:T(128)}, u32[]{:S(2)}) copy-start(f32[128]{0:T(128)} %copy-done.29) | copy-start | bytes 1540
  115.7 17.6 %copy-start.32 = (f32[128]{0:T(128)S(1)}, f32[128]{0:T(128)}, u32[]{:S(2)}) copy-start(f32[128]{0:T(128)} %copy-done.31) | copy-start | bytes 1540
  133.0 184.0 %all-reduce.3.cloned.1.call-start = ((), (), s32[]{:S(2)}) async-start(), calls=%async_computation.4 | async-start | bytes 14680064 | tf_op jit(solution)/shard_map/psum | solution.py:133
  150.4 2.3 copy-start.10
Sparse Core Ops, SparseCore 0:
  58.2 9.3 reduce-scatter.2
  133.1 9.1 reduce-scatter.4
  148.5 168.4 all-reduce.2
where the time goes:
time: 332 us; the launch traced here: 330 us
  waiting for transfers between devices  170 us (51%)
  local copies, waits for them, and re-layouts  51.5 us (16%)
  other arithmetic  51.2 us (15%)
  matrix products  26.3 us (8%)
  between operations  14.3 us (4%)
  starting transfers between devices  12 us (4%)
  blocking collectives  4.35 us (1%)
    psum x1, waiting for transfers between devices, body(): lax.psum((g_edge_first, g_edge_second, g_node_first, g_node_second), ('pa...  163 us
    unnamed x75, local copies, waits for them, and re-layouts  13.5 us
    ppermute x2, starting transfers between devices, padded(): lax.ppermute(lax.slice_in_dim(block, 0, width, axis=dim), axis, backward)  11.6 us
    dot_general x4, matrix products, contract_rows(): lax.dot_general(left, right, (((0,), (0,)), ((), ())), preferred_element_...  11.6 us
    scatter-add x1, other arithmetic, body(): jax.ops.segment_sum(d_edge[:, 2 * width:], receivers, num_segments=patch_...  9.24 us
    gather x2, local copies, waits for them, and re-layouts, body(): jnp.take(spread, receivers, axis=0)  7.76 us
    scatter-add x1, other arithmetic, body(): jax.ops.segment_sum(d_edge[:, width:2 * width], senders, num_segments=pat...  7.58 us
    dot_general x4, matrix products, times_transpose(): lax.dot_general(left, right, (((1,), (1,)), ((), ())), preferred_element_...  7.55 us
  transfers between devices with their start and end apart: 7, of which 2 were waited for; matrix products, arithmetic and copies ran while one was open for 15% of the time, Pallas kernels for 0%

commit v1 on v0

--- a/solution.py
+++ b/solution.py
@@ -1,9 +1,17 @@
+import functools
+
 import jax
 import jax.numpy as jnp
 from jax import lax
+from jax.experimental import pallas as pl
+from jax.experimental.pallas import tpu as pltpu
 from jax.sharding import PartitionSpec as P
 
 epsilon = 1e-05
+LANES = 128
+bf16 = jnp.bfloat16
+f32 = jnp.float32
+MESH = pl.DeviceIdType.MESH
 
 
 def padded(block, sides, width):
@@ -37,22 +45,36 @@
     )
 
 
-def mlp_forward(joined, w_first, w_second):
-    pre_act = jnp.dot(joined, w_first, preferred_element_type=jnp.float32)
-    activated = (pre_act * jax.nn.sigmoid(pre_act)).astype(jnp.bfloat16)
-    output = jnp.dot(activated, w_second, preferred_element_type=jnp.float32)
+def times(left, right):
+    return jnp.dot(left, right, preferred_element_type=jnp.float32)
+
+
+def layer_norm(output):
     center = output - jnp.mean(output, axis=-1, keepdims=True)
     inv_scale = lax.rsqrt(jnp.mean(center * center, axis=-1, keepdims=True) + epsilon)
-    return (pre_act, activated, center * inv_scale, inv_scale)
+    return center * inv_scale, inv_scale
+
+
+def norm_backward(cotangent, normed, inv_scale):
+    return (
+        inv_scale
+        * (
+            cotangent
+            - jnp.mean(cotangent, axis=-1, keepdims=True)
+            - normed * jnp.mean(cotangent * normed, axis=-1, keepdims=True)
+        )
+    ).astype(bf16)
+
+
+def mlp_forward(joined, w_first, w_second):
+    pre_act = times(joined, w_first)
+    activated = (pre_act * jax.nn.sigmoid(pre_act)).astype(jnp.bfloat16)
+    normed, inv_scale = layer_norm(times(activated, w_second))
+    return (pre_act, activated, normed, inv_scale)
 
 
 def mlp_backward(joined, w_first, w_second, pre_act, activated, normed, inv_scale, cotangent):
-    d_out = inv_scale * (
-        cotangent
-        - jnp.mean(cotangent, axis=-1, keepdims=True)
-        - normed * jnp.mean(cotangent * normed, axis=-1, keepdims=True)
-    )
-    d_out = d_out.astype(jnp.bfloat16)
+    d_out = norm_backward(cotangent, normed, inv_scale)
     d_act = times_transpose(d_out, w_second)
     d_pre = (d_act * swish_slope(pre_act)).astype(jnp.bfloat16)
     grad_second = contract_rows(activated, d_out)
@@ -61,7 +83,7 @@
     return (d_joined, grad_first, grad_second)
 
 
-def body(
+def general_body(
     node_latent,
     edge_latent,
     senders,
@@ -146,6 +168,376 @@
     return (grad_node_latent, grad_edge_latent, sliced[0], sliced[1], sliced[2], sliced[3])
 
 
+def rows_hot(index_row, count):
+    k = index_row.shape[1]
+    return (lax.broadcasted_iota(jnp.int32, (count, k), 0) == index_row).astype(f32).astype(bf16)
+
+
+def lanes_hot(index_row, count):
+    k = index_row.shape[1]
+    column = jnp.broadcast_to(index_row, (LANES, k)).T
+    lane = lax.broadcasted_iota(jnp.int32, (k, LANES), 1)
+    parts = [(column == lane + base).astype(f32).astype(bf16) for base in range(0, count, LANES)]
+    return jnp.concatenate(parts, axis=1)
+
+
+def make_plan(patches, width, units, tables):
+    bits = patches.bit_length() - 1
+    first = list(range(bits))
+    second = [1, 0] + first[2:]
+    third = first[2:] + [0, 1]
+    edge_cols = (tables["edge_first"] + tables["edge_second"]) // 2
+    node_cols = (tables["node_first"] + tables["node_second"]) // 2
+    def cut(total, share):
+        return total * share // 8 // LANES * LANES
+    a = cut(edge_cols, 3)
+    jobs = [
+        dict(group="edge", lo=0, hi=a, order=first),
+        dict(group="edge", lo=a, hi=2 * a, order=second),
+        dict(group="edge", lo=2 * a, hi=edge_cols, order=third),
+    ]
+    b = cut(node_cols, 4)
+    jobs += [
+        dict(group="node", lo=0, hi=b, order=first),
+        dict(group="node", lo=b, hi=node_cols, order=second),
+    ]
+    offset = 0
+    for job in jobs:
+        job["cols"] = job["hi"] - job["lo"]
+        job["out"] = offset
+        offset += job["cols"]
+    place = {
+        "edge_first": ("edge", 0),
+        "edge_second": ("edge", tables["edge_first"] // 2),
+        "node_first": ("node", 0),
+        "node_second": ("node", tables["node_first"] // 2),
+    }
+    return jobs, place, offset
+
+
+def fused_kernel(cfg, *refs):
+    patches, rows_out, chunk, steps = cfg["patches"], cfg["rows_out"], cfg["chunk"], cfg["steps"]
+    jobs, place, tables = cfg["jobs"], cfg["place"], cfg["tables"]
+    (node_ref, edge_ref, snd_ref, rcv_ref, halo_ref, a_ref, b_ref, na_ref, nb_ref, gn_ref, ge_ref) = refs[:11]
+    gnode_out, gedge_out, wsum_out = refs[11:14]
+    (ext, pre, act, normed, inv, dout, dpre, agg_acc, s_acc, r_acc,
+     halo_send, agg_send, agg_recv, spread, back_send, back_recv, own_acc, own_send, own_recv,
+     dnode, fin, send_sem, recv_sem) = refs[14:37]
+    buffers = refs[37:]
+
+    patch = lax.axis_index("patch")
+    core = lax.axis_index("shard")
+    other = 1 - core
+    nxt = lax.rem(patch + 1, patches)
+    prv = lax.rem(patch + patches - 1, patches)
+    node_rows, width = node_ref.shape
+    own = 2 * node_rows
+    halo = halo_send.shape[0] // 2
+    total = own + 2 * halo
+    bits = patches.bit_length() - 1
+
+    def bit_of(k):
+        return lax.rem(lax.div(patch, jnp.int32(1 << k)), jnp.int32(2))
+
+    def across(k):
+        return patch + (1 - 2 * bit_of(k)) * (1 << k)
+
+    greet = [(patch, other), (nxt, core), (prv, core)] + [(across(k), core) for k in range(bits)]
+    barrier = pltpu.get_barrier_semaphore()
+    for target in greet:
+        pl.semaphore_signal(barrier, inc=1, device_id=target, device_id_type=MESH)
+    pl.semaphore_wait(barrier, len(greet))
+
+    started = []
+
+    def send(src, dst, target):
+        k = len(started)
+        copy = pltpu.make_async_remote_copy(
+            src_ref=src, dst_ref=dst, send_sem=send_sem.at[k], recv_sem=recv_sem.at[k],
+            device_id=target, device_id_type=MESH,
+        )
+        copy.start()
+        started.append(copy)
+        return copy
+
+    state = []
+    at = 0
+    for job in jobs:
+        state.append(dict(job, bufs=buffers[at : at + 2 + bits], copy=None, step=0, base=None))
+        at += 2 + bits
+
+    def position(job, p):
+        return sum(((p >> b) & 1) << (bits - 1 - i) for i, b in enumerate(job["order"]))
+
+    def keep(name, first_col, value):
+        half = tables[name] // 2
+        group, offset = place[name]
+        value = value.astype(bf16)
+        for unit in range(0, value.shape[1], LANES):
+            column = first_col + unit
+            side, local = column // half, offset + column % half
+            for job in state:
+                if job["group"] == group and job["lo"] <= local < job["hi"]:
+                    lane = local - job["lo"]
+                    for p in range(patches):
+                        job["bufs"][0][side, position(job, p), :, lane : lane + LANES] = value[
+                            p * rows_out : (p + 1) * rows_out, unit : unit + LANES
+                        ]
+
+    def begin(group):
+        for job in state:
+            if job["group"] == group:
+                job["copy"] = send(job["bufs"][0].at[other], job["bufs"][1], (patch, other))
+                job["step"], job["base"] = 0, 0
+
+    def advance(group):
+        for job in state:
+            if job["group"] != group or job["step"] > bits:
+                continue
+            step, base, block = job["step"], job["base"], job["bufs"][0]
+            got = job["bufs"][1 + step]
+            job["copy"].wait_recv()
+            length = patches >> step
+            if step == bits:
+                value = block[core, base].astype(f32) + got[0].astype(f32)
+                fin[core, :, job["out"] : job["out"] + job["cols"]] = value
+            else:
+                half = length // 2
+                bit = bit_of(job["order"][step])
+                away, stay = (1 - bit) * half, bit * half
+
+                def add(start):
+                    where = pl.ds(base + start, half)
+                    block[core, where] = (
+                        block[core, where].astype(f32) + got[pl.ds(start, half)].astype(f32)
+                    ).astype(bf16)
+
+                add(away)
+                job["copy"] = send(
+                    block.at[core, pl.ds(base + away, half)],
+                    job["bufs"][2 + step],
+                    (across(job["order"][step]), core),
+                )
+                add(stay)
+                job["base"] = base + stay
+            job["step"] = step + 1
+
+    mine = pl.ds(pl.multiple_of(halo + core * node_rows, 16), node_rows)
+    ext[mine, :] = node_ref[...]
+    to_core = send(node_ref, ext.at[mine], (patch, other))
+    zero = jnp.zeros((own, width), f32)
+    agg_acc[...] = zero
+    r_acc[...] = zero
+    s_acc[...] = jnp.zeros((total, width), f32)
+    to_core.wait_recv()
+    inner = slice(halo, halo + own)
+    halo_send[...] = times(lanes_hot(halo_ref[...], own), ext[inner, :]).astype(bf16)
+    to_prev = send(halo_send.at[pl.ds(0, halo)], ext.at[pl.ds(halo + own, halo)], (prv, core))
+    to_next = send(halo_send.at[pl.ds(halo, halo)], ext.at[pl.ds(0, halo)], (nxt, core))
+
+    def rows_of(i):
+        return pl.ds(pl.multiple_of(i * chunk, chunk), chunk)
+
+    @pl.loop(0, steps)
+    def _(i):
+        rows = rows_of(i)
+        taken = times(lanes_hot(rcv_ref[i], own), ext[inner, :]).astype(bf16)
+        pre[rows, :] = times(edge_ref[rows, :], a_ref[:width, :]) + times(taken, a_ref[2 * width :, :])
+
+    to_prev.wait_recv()
+    to_next.wait_recv()
+
+    @pl.loop(0, steps)
+    def _(i):
+        rows = rows_of(i)
+        taken = times(lanes_hot(snd_ref[i], total), ext[...]).astype(bf16)
+        value = pre[rows, :] + times(taken, a_ref[width : 2 * width, :])
+        pre[rows, :] = value
+        hidden = (value * jax.nn.sigmoid(value)).astype(bf16)
+        act[rows, :] = hidden
+        scaled, scale = layer_norm(times(hidden, b_ref[...]))
+        normed[rows, :] = scaled
+        inv[rows, :] = scale
+        updated = (edge_ref[rows, :].astype(f32) + scaled).astype(bf16)
+        agg_acc[...] += times(rows_hot(rcv_ref[i], own), updated)
+
+    away_nodes = pl.ds(pl.multiple_of(other * node_rows, 16), node_rows)
+    own_nodes = pl.ds(pl.multiple_of(core * node_rows, 16), node_rows)
+    agg_send[...] = agg_acc[away_nodes, :].astype(bf16)
+    send(agg_send, agg_recv, (patch, other)).wait_recv()
+
+    node = node_ref[...]
+    aggregate = (agg_acc[own_nodes, :] + agg_recv[...].astype(f32)).astype(bf16)
+    n_pre = times(node, na_ref[:width, :]) + times(aggregate, na_ref[width:, :])
+    n_act = (n_pre * jax.nn.sigmoid(n_pre)).astype(bf16)
+    n_normed, n_inv = layer_norm(times(n_act, nb_ref[...]))
+    node_grad = gn_ref[...].astype(f32)
+    n_dout = norm_backward(node_grad, n_normed, n_inv)
+    n_dpre = (times_transpose(n_dout, nb_ref[...]) * swish_slope(n_pre)).astype(bf16)
+    spread[own_nodes, :] = times_transpose(n_dpre, na_ref[width:, :]).astype(bf16)
+    to_spread = send(spread.at[own_nodes], spread.at[own_nodes], (patch, other))
+    keep("node_first", 0, contract_rows(n_dpre, node))
+    keep("node_first", width, contract_rows(n_dpre, aggregate))
+    keep("node_second", 0, contract_rows(n_dout, n_act))
+    begin("node")
+    dnode[...] = node_grad + times_transpose(n_dpre, na_ref[:width, :])
+    to_spread.wait_recv()
+
+    def backward(i):
+        rows = rows_of(i)
+        cotangent = ge_ref[rows, :].astype(f32) + times(lanes_hot(rcv_ref[i], own), spread[...])
+        d_out = norm_backward(cotangent, normed[rows, :], inv[rows, :])
+        dout[rows, :] = d_out
+        d_pre = (times_transpose(d_out, b_ref[...]) * swish_slope(pre[rows, :])).astype(bf16)
+        dpre[rows, :] = d_pre
+        gedge_out[rows, :] = (cotangent + times_transpose(d_pre, a_ref[:width, :])).astype(bf16)
+        s_acc[...] += times(rows_hot(snd_ref[i], total), d_pre)
+        r_acc[...] += times(rows_hot(rcv_ref[i], own), d_pre)
+
+    pl.loop(0, steps // 2)(backward)
+    advance("node")
+    pl.loop(steps // 2, steps)(backward)
+    advance("node")
+
+    from_s = s_acc[...].astype(bf16)
+    from_r = r_acc[...].astype(bf16)
+    keep("edge_first", 0, contract_rows(dpre[...], edge_ref[...]))
+    keep("edge_first", width, contract_rows(from_s, ext[...]))
+    keep("edge_first", 2 * width, contract_rows(from_r, ext[inner, :]))
+    keep("edge_second", 0, contract_rows(dout[...], act[...]))
+    begin("edge")
+    advance("node")
+
+    back_send[:halo, :] = times_transpose(from_s[:halo, :], a_ref[width : 2 * width, :]).astype(bf16)
+    back_send[halo:, :] = times_transpose(from_s[halo + own :, :], a_ref[width : 2 * width, :]).astype(bf16)
+    back_prev = send(back_send.at[pl.ds(0, halo)], back_recv.at[pl.ds(halo, halo)], (prv, core))
+    back_next = send(back_send.at[pl.ds(halo, halo)], back_recv.at[pl.ds(0, halo)], (nxt, core))
+    advance("edge")
+    own_acc[...] = times_transpose(from_s[inner, :], a_ref[width : 2 * width, :]) + times_transpose(
+        from_r, a_ref[2 * width :, :]
+    )
+    back_prev.wait_recv()
+    back_next.wait_recv()
+    own_acc[...] += times(rows_hot(halo_ref[...], own), back_recv[...])
+    own_send[...] = own_acc[away_nodes, :].astype(bf16)
+    to_own = send(own_send, own_recv, (patch, other))
+    advance("node")
+    advance("edge")
+    to_own.wait_recv()
+    gnode_out[...] = (own_acc[own_nodes, :] + own_recv[...].astype(f32) + dnode[...]).astype(bf16)
+    for _ in range(bits + 1):
+        advance("node")
+        advance("edge")
+
+    send(fin.at[core], fin.at[core], (patch, other)).wait_recv()
+    wsum_out[...] = fin[...]
+    for copy in started:
+        copy.wait_send()
+
+
+def fused_body(
+    node_latent,
+    edge_latent,
+    senders,
+    receivers,
+    halo_list,
+    w_edge_first,
+    w_edge_second,
+    w_node_first,
+    w_node_second,
+    grad_node_new,
+    grad_edge_new,
+):
+    patches = lax.axis_size("patch")
+    edges, width = edge_latent.shape
+    node_rows = node_latent.shape[0]
+    units = w_edge_first.shape[1]
+    chunk = 256
+    steps = edges // chunk
+    halo2 = halo_list.shape[1]
+    own = 2 * node_rows
+    total = own + halo2
+    rows_out = units // patches
+    bits = patches.bit_length() - 1
+    tables = {
+        "edge_first": w_edge_first.shape[0],
+        "edge_second": w_edge_second.shape[0],
+        "node_first": w_node_first.shape[0],
+        "node_second": w_node_second.shape[0],
+    }
+    jobs, place, columns = make_plan(patches, width, units, tables)
+    cfg = dict(patches=patches, rows_out=rows_out, chunk=chunk, steps=steps, jobs=jobs, place=place, tables=tables)
+    job_bufs = []
+    for job in jobs:
+        shape = (rows_out, job["cols"])
+        job_bufs.append(pltpu.VMEM((2, patches) + shape, bf16))
+        job_bufs.append(pltpu.VMEM((patches,) + shape, bf16))
+        job_bufs += [pltpu.VMEM((patches >> (k + 1),) + shape, bf16) for k in range(bits)]
+    copies = 9 + len(jobs) * (bits + 1)
+    scratch = [
+        pltpu.VMEM((total, width), bf16),
+        pltpu.VMEM((edges, units), f32),
+        pltpu.VMEM((edges, units), bf16),
+        pltpu.VMEM((edges, width), f32),
+        pltpu.VMEM((edges, 1), f32),
+        pltpu.VMEM((edges, width), bf16),
+        pltpu.VMEM((edges, units), bf16),
+        pltpu.VMEM((own, width), f32),
+        pltpu.VMEM((total, units), f32),
+        pltpu.VMEM((own, units), f32),
+        pltpu.VMEM((halo2, width), bf16),
+        pltpu.VMEM((node_rows, width), bf16),
+        pltpu.VMEM((node_rows, width), bf16),
+        pltpu.VMEM((own, width), bf16),
+        pltpu.VMEM((halo2, width), bf16),
+        pltpu.VMEM((halo2, width), bf16),
+        pltpu.VMEM((own, width), f32),
+        pltpu.VMEM((node_rows, width), bf16),
+        pltpu.VMEM((node_rows, width), bf16),
+        pltpu.VMEM((node_rows, width), f32),
+        pltpu.VMEM((2, rows_out, columns), f32),
+        pltpu.SemaphoreType.DMA((copies,)),
+        pltpu.SemaphoreType.DMA((copies,)),
+    ] + job_bufs
+    vmem = pl.BlockSpec(memory_space=pltpu.VMEM)
+    gnode, gedge, wsum = pl.pallas_call(
+        functools.partial(fused_kernel, cfg),
+        out_shape=[
+            jax.ShapeDtypeStruct((node_rows, width), bf16),
+            jax.ShapeDtypeStruct((edges, width), bf16),
+            jax.ShapeDtypeStruct((2, rows_out, columns), f32),
+        ],
+        in_specs=[vmem] * 11,
+        out_specs=[vmem] * 3,
+        scratch_shapes=scratch,
+        compiler_params=pltpu.CompilerParams(
+            collective_id=0, has_side_effects=True, vmem_limit_bytes=52 * 1024 * 1024
+        ),
+        name="layer_backward",
+    )(
+        node_latent,
+        edge_latent,
+        senders.reshape(steps, 1, chunk),
+        receivers.reshape(steps, 1, chunk),
+        halo_list,
+        w_edge_first,
+        w_edge_second,
+        w_node_first,
+        w_node_second,
+        grad_node_new,
+        grad_edge_new,
+    )
+    base = {group: min(j["out"] for j in jobs if j["group"] == group) for group in ("edge", "node")}
+
+    def matrix(name):
+        group, offset = place[name]
+        low = base[group] + offset
+        part = wsum[:, :, low : low + tables[name] // 2]
+        return jnp.transpose(part, (0, 2, 1)).reshape(tables[name], rows_out)
+
+    return (gnode, gedge) + tuple(matrix(name) for name in ("edge_first", "edge_second", "node_first", "node_second"))
+
+
 def solution(mesh):
     in_specs = (
         P(("patch", "shard"), None),
@@ -168,4 +560,7 @@
         P(None, "patch"),
         P(None, "patch"),
     )
+    patches, shards = mesh.shape["patch"], mesh.shape["shard"]
+    covered = shards == 2 and patches >= 4 and patches & (patches - 1) == 0
+    body = fused_body if covered else general_body
     return jax.shard_map(body, mesh=mesh, in_specs=in_specs, out_specs=out_specs, check_vma=False)

time: 332 us -> 67.8 us (0.20)
  waiting for transfers between devices: 170 us -> 0 us
  Pallas kernels: 0 us -> 56.6 us
  other arithmetic: 51.2 us -> 0 us
  local copies, waits for them, and re-layouts: 51.5 us -> 10.2 us
  matrix products: 26.3 us -> 0 us
  between operations: 14.3 us -> 0.69 us
  starting transfers between devices: 12 us -> 0 us
  blocking collectives: 4.35 us -> 0 us
    psum x1 -> x0, waiting for transfers between devices: 163 us -> none  [body(): lax.psum((g_edge_first, g_edge_second, g_node_first, g_node_second), ('pa...]
    pallas_call x0 -> x1, Pallas kernels: none -> 56.6 us  [fused_body(): pl.pallas_call(functools.partial(fused_kernel, cfg), out_shape=[jax.Shape...]
    scatter-add x5 -> x0, other arithmetic: 30.4 us -> none  [the longest x1 9.24 us: body(): jax.ops.segment_sum(d_edge[:, 2 * width:], receivers, num_segments=patch_...]
    dot_general x12 -> x0, matrix products: 26.3 us -> none  [the longest x4 11.6 us: contract_rows(): lax.dot_general(left, right, (((0,), (0,)), ((), ())), preferred_element_...]
    gather x7 -> x0, local copies, waits for them, and re-layouts: 23.3 us -> none  [the longest x2 7.76 us: body(): jnp.take(spread, receivers, axis=0)]
    ppermute x4 -> x0, starting transfers between devices: 11.7 us -> none  [the longest x2 11.6 us: padded(): lax.ppermute(lax.slice_in_dim(block, 0, width, axis=dim), axis, backward)]
    convert_element_type x7 -> x0, other arithmetic: 10.5 us -> none  [the longest x1 3.82 us: body(): grad_edge_latent = (edge_grad + d_edge[:, :width]).astype(jnp.bfloat16)]
    reduce_scatter x2 -> x0, waiting for transfers between devices: 7.34 us -> none  [the longest x1 7.33 us: body(): lax.psum_scatter(partial_value.astype(jnp.bfloat16), 'shard', scatter_dim...]
  transfers between devices with their start and end apart: 7 -> 0, of which waited for: 2 -> 0; matrix products, arithmetic and copies ran while one was open for 15% -> 0% of each run, Pallas kernels for 0% -> 0%
where the time goes in v1:
time: 67.8 us; the launch traced here: 67.5 us
  Pallas kernels  56.6 us (83%)
  local copies, waits for them, and re-layouts  10.2 us (15%)
  between operations  0.69 us (1%)
    pallas_call x1, Pallas kernels, fused_body(): pl.pallas_call(functools.partial(fused_kernel, cfg), out_shape=[jax.Shape...  56.6 us
    unnamed x21, local copies, waits for them, and re-layouts  7.57 us
    reshape x4, local copies, waits for them, and re-layouts, matrix(): return jnp.transpose(part, (0, 2, 1)).reshape(tables[name], rows_out)  2.62 us

profile of v1, /device:TPU:1, one launch (start us, length us, event | category | flops | bytes accessed | tf_op | source)
XLA Modules:
  0.0 67.5 jit_solution(9571782582081757632)
XLA Ops:
  0.6 0.0 copy-start
  0.6 1.0 %copy-done = bf16[512,512]{1,0:T(8,128)(2,1)S(1)} copy-done((bf16[512,512]{1,0:T(8,128)(2,1)S(1)}, bf16[512,512]{1,0:T(8,128)(2,1)}, u32[]{:S(2)}) %copy-start) | copy-done | bytes 524312
  1.7 0.0 copy-start.1
  1.7 1.0 %copy-done.1 = bf16[512,512]{1,0:T(8,128)(2,1)S(1)} copy-done((bf16[512,512]{1,0:T(8,128)(2,1)S(1)}, bf16[512,512]{1,0:T(8,128)(2,1)}, u32[]{:S(2)}) %copy-start.1) | copy-done | bytes 524312
  2.7 0.0 copy-start.2
  2.7 0.9 %copy-done.2 = bf16[128,512]{1,0:T(8,128)(2,1)S(1)} copy-done((bf16[128,512]{1,0:T(8,128)(2,1)S(1)}, bf16[128,512]{1,0:T(8,128)(2,1)}, u32[]{:S(2)}) %copy-start.2) | copy-done | bytes 131096
  3.6 0.0 copy-start.3
  3.6 0.9 %copy-done.3 = bf16[128,512]{1,0:T(8,128)(2,1)S(1)} copy-done((bf16[128,512]{1,0:T(8,128)(2,1)S(1)}, bf16[128,512]{1,0:T(8,128)(2,1)}, u32[]{:S(2)}) %copy-start.3) | copy-done | bytes 131096
  4.5 0.0 copy-start.4
  4.5 0.7 %copy-done.4 = s32[1024]{0:T(1024)S(1)} copy-done((s32[1024]{0:T(1024)S(1)}, s32[1024]{0:T(1024)}, u32[]{:S(2)}) %copy-start.4) | copy-done | bytes 4120
  5.2 0.0 copy-start.5
  5.2 0.7 %copy-done.5 = s32[1024]{0:T(1024)S(1)} copy-done((s32[1024]{0:T(1024)S(1)}, s32[1024]{0:T(1024)}, u32[]{:S(2)}) %copy-start.5) | copy-done | bytes 4120
  5.9 0.0 copy-start.6
  5.9 0.7 copy-done.6
  6.6 56.6 %layer_backward.1 = (bf16[128,512]{1,0:T(8,128)(2,1)S(1)}, bf16[1024,512]{1,0:T(8,128)(2,1)}, f32[2,32,1792]{2,1,0:T(8,128)S(1)}) custom-call(bf16[128,512]{1,0:T(8,128)(2,1)S(1)} %copy-done.2, bf16[1024,512]{1,0:T(8,128)(2,1)} %refs_1_.1, s32[4,1,256]{2,1,0:T(1,128)S(1)} %bitcast.18, s32[4,1,256]{2,1,0:T(1,128)S(1)} %bitcast.19, s32[1,128]{1,0:T(1,128)S(1)} %copy-done.6, ...), custom_call_target="tpu_custom_call" | custom-call | tf_op jit(solution)/shard_map/layer_backward/pallas_call | solution.py:503
  63.2 0.0 copy-start.7
  63.2 0.7 copy.23
  63.9 0.7 %copy.21 = f32[2,4,8,768]{3,2,0,1:T(8,128)} copy(f32[2,4,8,768]{3,2,1,0:T(8,128)S(1)} %slice_bitcast_fusion) | data formatting | bytes 393216 | tf_op jit(solution)/shard_map/reshape | solution.py:536
  64.6 0.6 copy.24
  65.3 0.6 copy.22
  65.9 0.7 copy.27
  66.5 0.0 copy-done.7
  66.5 1.0 %copy.28 = bf16[1024,512]{1,0:T(8,128)(2,1)} copy(bf16[1024,512]{1,0:T(8,128)(2,1)S(1)} %copy-done.7) | data formatting | bytes 2097152
  (3 shorter events, 0.0 us)
Async XLA Ops:
  0.6 1.0 %copy-start = (bf16[512,512]{1,0:T(8,128)(2,1)S(1)}, bf16[512,512]{1,0:T(8,128)(2,1)}, u32[]{:S(2)}) copy-start(bf16[512,512]{1,0:T(8,128)(2,1)} %refs_6_.1) | copy-start | bytes 1572868
  1.7 1.0 %copy-start.1 = (bf16[512,512]{1,0:T(8,128)(2,1)S(1)}, bf16[512,512]{1,0:T(8,128)(2,1)}, u32[]{:S(2)}) copy-start(bf16[512,512]{1,0:T(8,128)(2,1)} %refs_8_.1) | copy-start | bytes 1572868
  2.7 0.9 %copy-start.2 = (bf16[128,512]{1,0:T(8,128)(2,1)S(1)}, bf16[128,512]{1,0:T(8,128)(2,1)}, u32[]{:S(2)}) copy-start(bf16[128,512]{1,0:T(8,128)(2,1)} %refs_0_.1) | copy-start | bytes 393220
  3.6 0.9 %copy-start.3 = (bf16[128,512]{1,0:T(8,128)(2,1)S(1)}, bf16[128,512]{1,0:T(8,128)(2,1)}, u32[]{:S(2)}) copy-start(bf16[128,512]{1,0:T(8,128)(2,1)} %refs_9_.1) | copy-start | bytes 393220
  4.5 0.7 %copy-start.4 = (s32[1024]{0:T(1024)S(1)}, s32[1024]{0:T(1024)}, u32[]{:S(2)}) copy-start(s32[1024]{0:T(1024)} %param.13) | copy-start | bytes 12292
  5.2 0.7 %copy-start.5 = (s32[1024]{0:T(1024)S(1)}, s32[1024]{0:T(1024)}, u32[]{:S(2)}) copy-start(s32[1024]{0:T(1024)} %param.14) | copy-start | bytes 12292
  5.9 0.7 copy-start.6
  63.2 3.3 %copy-start.7 = (bf16[1024,512]{1,0:T(8,128)(2,1)S(1)}, bf16[1024,512]{1,0:T(8,128)(2,1)}, u32[]{:S(2)}) copy-start(bf16[1024,512]{1,0:T(8,128)(2,1)} %get-tuple-element.21) | copy-start | bytes 3145732

commit v2 on v1

v2 whole, which is shorter than its diff:
```python
import functools

import jax
import jax.numpy as jnp
from jax import lax
from jax.experimental import pallas as pl
from jax.experimental.pallas import tpu as pltpu
from jax.sharding import PartitionSpec as P

epsilon = 1e-05
LANES = 128
bf16 = jnp.bfloat16
f32 = jnp.float32
MESH = pl.DeviceIdType.MESH


def padded(block, sides, width):
    for axis, dim in sides:
        count = lax.axis_size(axis)
        forward = [(i, i + 1) for i in range(count - 1)]
        forward.append((count - 1, 0))
        backward = [(target, source) for source, target in forward]
        low = lax.ppermute(
            lax.slice_in_dim(block, block.shape[dim] - width, None, axis=dim), axis, forward
        )
        high = lax.ppermute(lax.slice_in_dim(block, 0, width, axis=dim), axis, backward)
        block = jnp.concatenate([low, block, high], axis=dim)
    return block


def swish_slope(values):
    sig = jax.nn.sigmoid(values)
    return sig * (1.0 + values * (1.0 - sig))


def contract_rows(left, right):
    return lax.dot_general(
        left, right, (((0,), (0,)), ((), ())), preferred_element_type=jnp.float32
    )


def times_transpose(left, right):
    return lax.dot_general(
        left, right, (((1,), (1,)), ((), ())), preferred_element_type=jnp.float32
    )


def times(left, right):
    return jnp.dot(left, right, preferred_element_type=jnp.float32)


def layer_norm(output):
    center = output - jnp.mean(output, axis=-1, keepdims=True)
    inv_scale = lax.rsqrt(jnp.mean(center * center, axis=-1, keepdims=True) + epsilon)
    return center * inv_scale, inv_scale


def norm_backward(cotangent, normed, inv_scale):
    return (
        inv_scale
        * (
            cotangent
            - jnp.mean(cotangent, axis=-1, keepdims=True)
            - normed * jnp.mean(cotangent * normed, axis=-1, keepdims=True)
        )
    ).astype(bf16)


def mlp_forward(joined, w_first, w_second):
    pre_act = times(joined, w_first)
    activated = (pre_act * jax.nn.sigmoid(pre_act)).astype(jnp.bfloat16)
    normed, inv_scale = layer_norm(times(activated, w_second))
    return (pre_act, activated, normed, inv_scale)


def mlp_backward(joined, w_first, w_second, pre_act, activated, normed, inv_scale, cotangent):
    d_out = norm_backward(cotangent, normed, inv_scale)
    d_act = times_transpose(d_out, w_second)
    d_pre = (d_act * swish_slope(pre_act)).astype(jnp.bfloat16)
    grad_second = contract_rows(activated, d_out)
    grad_first = contract_rows(joined, d_pre)
    d_joined = times_transpose(d_pre, w_first)
    return (d_joined, grad_first, grad_second)


def general_body(
    node_latent,
    edge_latent,
    senders,
    receivers,
    halo_list,
    w_edge_first,
    w_edge_second,
    w_node_first,
    w_node_second,
    grad_node_new,
    grad_edge_new,
):
    shards = lax.axis_size("shard")
    node_rows = node_latent.shape[0]
    width = node_latent.shape[1]
    patch_rows = node_rows * shards
    send_lists = halo_list[0]
    halo_width = send_lists.shape[0] // 2
    gathered = lax.all_gather(node_latent, "shard", axis=0, tiled=True)
    outgoing = jnp.take(gathered, send_lists, axis=0)
    widened = padded(outgoing, (("patch", 0),), halo_width)
    from_prev = widened[:halo_width]
    from_next = widened[halo_width * 3 :]
    extended = jnp.concatenate([from_prev, gathered, from_next], axis=0)
    joined = jnp.concatenate(
        [edge_latent, jnp.take(extended, senders, axis=0), jnp.take(gathered, receivers, axis=0)],
        axis=1,
    )
    pre_act, activated, normed, inv_scale = mlp_forward(joined, w_edge_first, w_edge_second)
    edge_new = (edge_latent.astype(jnp.float32) + normed).astype(jnp.bfloat16)
    partial_value = jax.ops.segment_sum(
        edge_new.astype(jnp.float32), receivers, num_segments=patch_rows
    )
    aggregate = lax.psum_scatter(
        partial_value.astype(jnp.bfloat16), "shard", scatter_dimension=0, tiled=True
    )
    node_joined = jnp.concatenate([node_latent, aggregate], axis=1)
    n_pre, n_act, n_normed, n_inv = mlp_forward(node_joined, w_node_first, w_node_second)
    node_grad = grad_node_new.astype(jnp.float32)
    d_node, g_node_first, g_node_second = mlp_backward(
        node_joined, w_node_first, w_node_second, n_pre, n_act, n_normed, n_inv, node_grad
    )
    d_aggregate = d_node[:, width:]
    spread = lax.all_gather(d_aggregate.astype(jnp.bfloat16), "shard", axis=0, tiled=True).astype(
        d_aggregate.dtype
    )
    edge_grad = grad_edge_new.astype(jnp.float32) + jnp.take(spread, receivers, axis=0)
    d_edge, g_edge_first, g_edge_second = mlp_backward(
        joined, w_edge_first, w_edge_second, pre_act, activated, normed, inv_scale, edge_grad
    )
    grad_edge_latent = (edge_grad + d_edge[:, :width]).astype(jnp.bfloat16)
    sender_part = jax.ops.segment_sum(
        d_edge[:, width : 2 * width], senders, num_segments=patch_rows + 2 * halo_width
    )
    receiver_part = jax.ops.segment_sum(d_edge[:, 2 * width :], receivers, num_segments=patch_rows)
    back_part = jnp.concatenate(
        [sender_part[:halo_width], sender_part[halo_width + patch_rows :]], axis=0
    )
    returned = padded(back_part.astype(jnp.bfloat16), (("patch", 0),), halo_width).astype(
        back_part.dtype
    )
    own_rows = sender_part[halo_width : halo_width + patch_rows] + receiver_part
    own_rows = own_rows.at[send_lists[:halo_width]].add(returned[:halo_width])
    own_rows = own_rows.at[send_lists[halo_width:]].add(returned[halo_width * 3 :])
    node_total = lax.psum_scatter(
        own_rows.astype(jnp.bfloat16), "shard", scatter_dimension=0, tiled=True
    ).astype(jnp.float32)
    grad_node_latent = (node_total + node_grad + d_node[:, :width]).astype(jnp.bfloat16)
    summed = lax.psum(
        (g_edge_first, g_edge_second, g_node_first, g_node_second), ("patch", "shard")
    )
    patches = lax.axis_size("patch")
    patch_index = lax.axis_index("patch")
    sliced = tuple(
        (
            lax.dynamic_slice_in_dim(
                matrix, patch_index * (matrix.shape[1] // patches), matrix.shape[1] // patches, 1
            )
            for matrix in summed
        )
    )
    return (grad_node_latent, grad_edge_latent, sliced[0], sliced[1], sliced[2], sliced[3])


def rows_hot(index_row, count):
    k = index_row.shape[1]
    return (lax.broadcasted_iota(jnp.int32, (count, k), 0) == index_row).astype(f32).astype(bf16)


def lanes_hot(index_row, count):
    k = index_row.shape[1]
    column = jnp.broadcast_to(index_row, (LANES, k)).T
    lane = lax.broadcasted_iota(jnp.int32, (k, LANES), 1)
    parts = [(column == lane + base).astype(f32).astype(bf16) for base in range(0, count, LANES)]
    return jnp.concatenate(parts, axis=1)


JOBS = ("node_first", "node_first", "node_second", "edge_second", "edge_first", "edge_first", "edge_first")


def make_orders(bits):
    upper = list(range(2, bits))
    first = [0, 1] + upper
    second = [1, 0] + upper
    third = upper + [0, 1]
    return (first, second, first, third, first, second, second)


def fused_kernel(cfg, *refs):
    patches, rows_out, half, chunk = cfg["patches"], cfg["rows_out"], cfg["half"], cfg["chunk"]
    (node_hbm, edge_hbm, snd_ref, rcv_ref, halo_ref, a_hbm, b_hbm, na_hbm, nb_hbm, gn_hbm, ge_hbm) = refs[:11]
    gnode_out, gedge_hbm, wsum_out = refs[11:14]
    (edge_ref, a_ref, b_ref, na_ref, nb_ref, gn_ref, ge_ref,
     ext, hot_s, hot_r, pre, act, normed, inv, cot, dout, dpre, dpre_t, updated, gedge,
     halo_send, agg_send, agg_recv, agg, n_dpre, n_dout, n_act, spread, dnode,
     back_send, back_recv, own_acc, own_send, own_recv, fin,
     in_sem, out_sem, send_sem, recv_sem) = refs[14:53]
    buffers = refs[53:]

    patch = lax.axis_index("patch")
    core = lax.axis_index("shard")
    other = 1 - core
    nxt = lax.rem(patch + 1, patches)
    prv = lax.rem(patch + patches - 1, patches)
    node_rows, width = node_hbm.shape
    edges = edge_hbm.shape[0]
    own = 2 * node_rows
    halo = halo_send.shape[0] // 2
    total = own + 2 * halo
    bits = patches.bit_length() - 1
    chunks = [slice(i, i + chunk) for i in range(0, edges, chunk)]

    def bit_of(k):
        return lax.rem(lax.div(patch, jnp.int32(1 << k)), jnp.int32(2))

    def across(k):
        return patch + (1 - 2 * bit_of(k)) * (1 << k)

    greet = [(patch, other), (nxt, core), (prv, core)] + [(across(k), core) for k in range(bits)]
    barrier = pltpu.get_barrier_semaphore()
    for target in greet:
        pl.semaphore_signal(barrier, inc=1, device_id=target, device_id_type=MESH)

    mine = pl.ds(pl.multiple_of(halo + core * node_rows, 16), node_rows)
    own_nodes = pl.ds(pl.multiple_of(core * node_rows, 16), node_rows)
    away_nodes = pl.ds(pl.multiple_of(other * node_rows, 16), node_rows)
    inner = slice(halo, halo + own)

    loads = {}
    for k, (name, src, dst) in enumerate(
        (
            ("node", node_hbm, ext.at[mine]),
            ("edge", edge_hbm, edge_ref),
            ("a", a_hbm, a_ref),
            ("b", b_hbm, b_ref),
            ("gn", gn_hbm, gn_ref.at[own_nodes]),
            ("na", na_hbm, na_ref),
            ("nb", nb_hbm, nb_ref),
            ("ge", ge_hbm, ge_ref),
        )
    ):
        loads[name] = pltpu.make_async_copy(src, dst, in_sem.at[k])
        loads[name].start()

    pl.semaphore_wait(barrier, len(greet))

    started = []

    def send(src, dst, target):
        k = len(started)
        copy = pltpu.make_async_remote_copy(
            src_ref=src, dst_ref=dst, send_sem=send_sem.at[k], recv_sem=recv_sem.at[k],
            device_id=target, device_id_type=MESH,
        )
        copy.start()
        started.append(copy)
        return copy

    to_core = send(node_hbm, ext.at[mine], (patch, other))
    to_core_grad = send(gn_hbm, gn_ref.at[own_nodes], (patch, other))

    state = []
    for k, order in enumerate(make_orders(bits)):
        bufs = buffers[k * (2 + bits) : (k + 1) * (2 + bits)]
        state.append(dict(order=order, bufs=bufs, copy=None, step=0, base=0, out=k * half))

    def gradient(k, left_t, right):
        job = state[k]
        block = job["bufs"][0]
        for side in (other, core):
            lanes = pl.ds(pl.multiple_of(side * half, LANES), half)
            value = times(left_t, right(lanes)).astype(bf16)
            for p in range(patches):
                where = sum(((p >> b) & 1) << (bits - 1 - i) for i, b in enumerate(job["order"]))
                block[side, where] = value[p * rows_out : (p + 1) * rows_out]
            if side is other:
                job["copy"] = send(block.at[other], job["bufs"][1], (patch, other))

    def advance(*ks):
        for k in ks:
            job = state[k]
            step, base, block = job["step"], job["base"], job["bufs"][0]
            if step > bits:
                continue
            got = job["bufs"][1 + step]
            job["copy"].wait_recv()
            if step == bits:
                value = block[core, base].astype(f32) + got[0].astype(f32)
                fin[core, :, job["out"] : job["out"] + half] = value
            else:
                count = (patches >> step) // 2
                bit = bit_of(job["order"][step])
                away, stay = (1 - bit) * count, bit * count

                def add(start):
                    where = pl.ds(base + start, count)
                    block[core, where] = (
                        block[core, where].astype(f32) + got[pl.ds(start, count)].astype(f32)
                    ).astype(bf16)

                add(away)
                job["copy"] = send(
                    block.at[core, pl.ds(base + away, count)],
                    job["bufs"][2 + step],
                    (across(job["order"][step]), core),
                )
                add(stay)
                job["base"] = base + stay
            job["step"] = step + 1

    hot_r[...] = lanes_hot(rcv_ref[...], own)
    loads["edge"].wait()
    loads["a"].wait()
    for rows in chunks:
        pre[rows, :] = times(edge_ref[rows, :], a_ref[:width, :])
    loads["node"].wait()
    to_core.wait_recv()
    halo_send[...] = times(lanes_hot(halo_ref[...], own), ext[inner, :]).astype(bf16)
    to_prev = send(halo_send.at[pl.ds(0, halo)], ext.at[pl.ds(halo + own, halo)], (prv, core))
    to_next = send(halo_send.at[pl.ds(halo, halo)], ext.at[pl.ds(0, halo)], (nxt, core))

    for rows in chunks:
        taken = times(hot_r[rows, :], ext[inner, :]).astype(bf16)
        pre[rows, :] += times(taken, a_ref[2 * width :, :])
    hot_s[...] = lanes_hot(snd_ref[...], total)
    loads["b"].wait()
    to_prev.wait_recv()
    to_next.wait_recv()
    for rows in chunks:
        taken = times(hot_s[rows, :], ext[...]).astype(bf16)
        value = pre[rows, :] + times(taken, a_ref[width : 2 * width, :])
        pre[rows, :] = value
        hidden = (value * jax.nn.sigmoid(value)).astype(bf16)
        act[rows, :] = hidden
        scaled, scale = layer_norm(times(hidden, b_ref[...]))
        normed[rows, :] = scaled
        inv[rows, :] = scale
        updated[rows, :] = (edge_ref[rows, :].astype(f32) + scaled).astype(bf16)
    agg_send[...] = times(rows_hot(rcv_ref[...], own), updated[...]).astype(bf16)
    to_agg = send(agg_send, agg_recv, (patch, other))

    @pl.loop(0, edges // LANES)
    def _(i):
        rows = pl.ds(pl.multiple_of(i * LANES, LANES), LANES)
        pre[rows, :] = swish_slope(pre[rows, :])

    for name in ("na", "nb", "gn", "ge"):
        loads[name].wait()
    to_core_grad.wait_recv()
    to_agg.wait_recv()

    node = ext[inner, :]
    aggregate = (agg_send[...].astype(f32) + agg_recv[...].astype(f32)).astype(bf16)
    agg[...] = aggregate
    n_pre = times(node, na_ref[:width, :]) + times(aggregate, na_ref[width:, :])
    hidden = (n_pre * jax.nn.sigmoid(n_pre)).astype(bf16)
    n_act[...] = hidden
    n_normed, n_inv = layer_norm(times(hidden, nb_ref[...]))
    d_out = norm_backward(gn_ref[...].astype(f32), n_normed, n_inv)
    n_dout[...] = d_out
    d_pre = (times_transpose(d_out, nb_ref[...]) * swish_slope(n_pre)).astype(bf16)
    n_dpre[...] = d_pre
    spread[...] = times_transpose(d_pre, na_ref[width:, :]).astype(bf16)

    n_dpre_own = n_dpre[own_nodes, :]
    n_dpre_t = n_dpre_own.T
    gradient(0, n_dpre_t, lambda lanes: ext[mine, lanes])
    gradient(1, n_dpre_t, lambda lanes: agg[own_nodes, lanes])
    gradient(2, n_dout[own_nodes, :].T, lambda lanes: n_act[own_nodes, lanes])

    for rows in chunks:
        cotangent = ge_ref[rows, :].astype(f32) + times(hot_r[rows, :], spread[...])
        cot[rows, :] = cotangent
        dout[rows, :] = norm_backward(cotangent, normed[rows, :], inv[rows, :])
    advance(0, 1, 2)
    gradient(3, dout[...].T, lambda lanes: act[:, lanes])
    for rows in chunks:
        dpre[rows, :] = (times_transpose(dout[rows, :], b_ref[...]) * pre[rows, :]).astype(bf16)
    dpre_t[...] = dpre[...].T
    advance(3)
    gradient(4, dpre_t[...], lambda lanes: edge_ref[:, lanes])
    from_s_t = times(dpre_t[...], hot_s[...]).astype(bf16)
    gradient(5, from_s_t, lambda lanes: ext[:, lanes])
    from_r_t = times(dpre_t[...], hot_r[...]).astype(bf16)
    gradient(6, from_r_t, lambda lanes: ext[inner, lanes])
    advance(4, 0, 1, 2)

    from_s = from_s_t.T
    from_r = from_r_t.T
    back_send[:halo, :] = times_transpose(from_s[:halo, :], a_ref[width : 2 * width, :]).astype(bf16)
    back_send[halo:, :] = times_transpose(from_s[halo + own :, :], a_ref[width : 2 * width, :]).astype(bf16)
    back_prev = send(back_send.at[pl.ds(0, halo)], back_recv.at[pl.ds(halo, halo)], (prv, core))
    back_next = send(back_send.at[pl.ds(halo, halo)], back_recv.at[pl.ds(0, halo)], (nxt, core))
    advance(5, 6)
    stores = []

    def edge_rows(k):
        rows = chunks[k]
        gedge[rows, :] = (cot[rows, :] + times_transpose(dpre[rows, :], a_ref[:width, :])).astype(bf16)
        stores.append(pltpu.make_async_copy(gedge.at[rows], gedge_hbm.at[rows], out_sem.at[k]))
        stores[-1].start()

    split = len(chunks) // 2
    for k in range(split):
        edge_rows(k)
    advance(3, 4, 0, 1, 2)
    for k in range(split, len(chunks)):
        edge_rows(k)
    own_acc[...] = times_transpose(from_s[inner, :], a_ref[width : 2 * width, :]) + times_transpose(
        from_r, a_ref[2 * width :, :]
    )
    dnode[...] = gn_ref[own_nodes, :].astype(f32) + times_transpose(n_dpre_own, na_ref[:width, :])
    advance(5, 6, 3, 4)
    back_prev.wait_recv()
    back_next.wait_recv()
    own_acc[...] += times(rows_hot(halo_ref[...], own), back_recv[...])
    own_send[...] = own_acc[away_nodes, :].astype(bf16)
    to_own = send(own_send, own_recv, (patch, other))
    advance(5, 6, 0, 1, 2, 3, 4)
    to_own.wait_recv()
    gnode_out[...] = (own_acc[own_nodes, :] + own_recv[...].astype(f32) + dnode[...]).astype(bf16)
    for _ in range(bits):
        advance(0, 1, 2, 3, 4, 5, 6)

    send(fin.at[core], fin.at[core], (patch, other)).wait_recv()
    wsum_out[...] = fin[...]
    for copy in stores:
        copy.wait()
    for copy in started:
        copy.wait_send()


def finish_kernel(half, gnode_ref, gedge_ref, wsum_ref, gnode_out, gedge_out, e1, e2, n1, n2, sem):
    copies = [(gedge_ref, gedge_out), (gnode_ref, gnode_out)]
    outs = {"edge_first": e1, "edge_second": e2, "node_first": n1, "node_second": n2}
    seen = {name: 0 for name in outs}
    for k, name in enumerate(JOBS):
        for side in range(2):
            low = seen[name] + side * half
            copies.append((wsum_ref.at[side, :, k * half : (k + 1) * half], outs[name].at[:, low : low + half]))
        seen[name] += 2 * half
    copies = [pltpu.make_async_copy(src, dst, sem.at[k]) for k, (src, dst) in enumerate(copies)]
    for copy in copies:
        copy.start()
    for copy in copies:
        copy.wait()


def fused_body(
    node_latent,
    edge_latent,
    senders,
    receivers,
    halo_list,
    w_edge_first,
    w_edge_second,
    w_node_first,
    w_node_second,
    grad_node_new,
    grad_edge_new,
):
    patches = lax.axis_size("patch")
    edges, width = edge_latent.shape
    node_rows = node_latent.shape[0]
    units = w_edge_first.shape[1]
    half = width // 2
    chunk = edges // 2
    halo2 = halo_list.shape[1]
    own = 2 * node_rows
    total = own + halo2
    rows_out = units // patches
    bits = patches.bit_length() - 1
    cfg = dict(patches=patches, rows_out=rows_out, half=half, chunk=chunk)
    job_bufs = []
    for _ in JOBS:
        shape = (rows_out, half)
        job_bufs.append(pltpu.VMEM((2, patches) + shape, bf16))
        job_bufs.append(pltpu.VMEM((patches,) + shape, bf16))
        job_bufs += [pltpu.VMEM((patches >> (k + 1),) + shape, bf16) for k in range(bits)]
    copies = 9 + len(JOBS) * (bits + 1)
    scratch = [
        pltpu.VMEM(edge_latent.shape, bf16),
        pltpu.VMEM(w_edge_first.shape, bf16),
        pltpu.VMEM(w_edge_second.shape, bf16),
        pltpu.VMEM(w_node_first.shape, bf16),
        pltpu.VMEM(w_node_second.shape, bf16),
        pltpu.VMEM((own, width), bf16),
        pltpu.VMEM((edges, width), bf16),
        pltpu.VMEM((total, width), bf16),
        pltpu.VMEM((edges, total), bf16),
        pltpu.VMEM((edges, own), bf16),
        pltpu.VMEM((edges, units), f32),
        pltpu.VMEM((edges, units), bf16),
        pltpu.VMEM((edges, width), f32),
        pltpu.VMEM((edges, 1), f32),
        pltpu.VMEM((edges, width), f32),
        pltpu.VMEM((edges, width), bf16),
        pltpu.VMEM((edges, units), bf16),
        pltpu.VMEM((units, edges), bf16),
        pltpu.VMEM((edges, width), bf16),
        pltpu.VMEM((edges, width), bf16),
        pltpu.VMEM((halo2, width), bf16),
        pltpu.VMEM((own, width), bf16),
        pltpu.VMEM((own, width), bf16),
        pltpu.VMEM((own, width), bf16),
        pltpu.VMEM((own, units), bf16),
        pltpu.VMEM((own, width), bf16),
        pltpu.VMEM((own, units), bf16),
        pltpu.VMEM((own, width), bf16),
        pltpu.VMEM((node_rows, width), f32),
        pltpu.VMEM((halo2, width), bf16),
        pltpu.VMEM((halo2, width), bf16),
        pltpu.VMEM((own, width), f32),
        pltpu.VMEM((node_rows, width), bf16),
        pltpu.VMEM((node_rows, width), bf16),
        pltpu.VMEM((2, rows_out, len(JOBS) * half), f32),
        pltpu.SemaphoreType.DMA((8,)),
        pltpu.SemaphoreType.DMA((edges // chunk,)),
        pltpu.SemaphoreType.DMA((copies,)),
        pltpu.SemaphoreType.DMA((copies,)),
    ] + job_bufs
    vmem = pl.BlockSpec(memory_space=pltpu.VMEM)
    hbm = pl.BlockSpec(memory_space=pltpu.HBM)
    anywhere = pl.BlockSpec(memory_space=pl.ANY)
    gnode, gedge, wsum = pl.pallas_call(
        functools.partial(fused_kernel, cfg),
        out_shape=[
            jax.ShapeDtypeStruct((node_rows, width), bf16),
            jax.ShapeDtypeStruct((edges, width), bf16),
            jax.ShapeDtypeStruct((2, rows_out, len(JOBS) * half), f32),
        ],
        in_specs=[hbm, hbm, vmem, vmem, vmem] + [hbm] * 6,
        out_specs=[vmem, anywhere, vmem],
        scratch_shapes=scratch,
        compiler_params=pltpu.CompilerParams(
            collective_id=0, has_side_effects=True, vmem_limit_bytes=56 * 1024 * 1024
        ),
        name="layer_backward",
    )(
        node_latent,
        edge_latent,
        senders.reshape(1, edges),
        receivers.reshape(1, edges),
        halo_list,
        w_edge_first,
        w_edge_second,
        w_node_first,
        w_node_second,
        grad_node_new,
        grad_edge_new,
    )
    matrices = (w_edge_first, w_edge_second, w_node_first, w_node_second)
    gnode, gedge, *parts = pl.pallas_call(
        functools.partial(finish_kernel, half),
        out_shape=[
            jax.ShapeDtypeStruct((node_rows, width), bf16),
            jax.ShapeDtypeStruct((edges, width), bf16),
        ]
        + [jax.ShapeDtypeStruct((rows_out, m.shape[0]), f32) for m in matrices],
        in_specs=[anywhere] * 3,
        out_specs=[hbm] * 6,
        scratch_shapes=[pltpu.SemaphoreType.DMA((2 + 2 * len(JOBS),))],
        name="results",
    )(gnode, gedge, wsum)
    return (gnode, gedge) + tuple(part.T for part in parts)


def solution(mesh):
    in_specs = (
        P(("patch", "shard"), None),
        P(("patch", "shard"), None),
        P(("patch", "shard")),
        P(("patch", "shard")),
        P("patch", None),
        P(),
        P(),
        P(),
        P(),
        P(("patch", "shard"), None),
        P(("patch", "shard"), None),
    )
    out_specs = (
        P(("patch", "shard"), None),
        P(("patch", "shard"), None),
        P(None, "patch"),
        P(None, "patch"),
        P(None, "patch"),
        P(None, "patch"),
    )
    patches, shards = mesh.shape["patch"], mesh.shape["shard"]
    covered = shards == 2 and patches >= 4 and patches & (patches - 1) == 0
    body = fused_body if covered else general_body
    return jax.shard_map(body, mesh=mesh, in_specs=in_specs, out_specs=out_specs, check_vma=False)
```

time: 67.8 us -> 103 us (1.52)
  Pallas kernels: 56.6 us -> 102 us
  local copies, waits for them, and re-layouts: 10.2 us -> 0 us
    pallas_call x0 -> x1, Pallas kernels: none -> 50.9 us  [fused_body(): pl.pallas_call(functools.partial(finish_kernel, half), out_shape=[jax.Sha...]
    unnamed x21 -> x0, local copies, waits for them, and re-layouts: 7.57 us -> none
    pallas_call x1, Pallas kernels: 56.6 us -> 51.6 us  [fused_body(): pl.pallas_call(functools.partial(fused_kernel, cfg), out_shape=[jax.Shape...]
    reshape x4 -> x0, local copies, waits for them, and re-layouts: 2.62 us -> none  [matrix(): return jnp.transpose(part, (0, 2, 1)).reshape(tables[name], rows_out)]
where the time goes in v2:
time: 103 us
  Pallas kernels  102 us (99%)
    pallas_call x1, Pallas kernels, fused_body(): pl.pallas_call(functools.partial(fused_kernel, cfg), out_shape=[jax.Shape...  51.6 us
    pallas_call x1, Pallas kernels, fused_body(): pl.pallas_call(functools.partial(finish_kernel, half), out_shape=[jax.Sha...  50.9 us

profile of v2, /device:TPU:1, one launch (start us, length us, event | category | flops | bytes accessed | tf_op | source)
XLA Modules:
  0.0 103.3 jit_solution(8765994624728168090)
XLA Ops:
  0.6 51.6 %layer_backward.1 = (bf16[128,512]{1,0:T(8,128)(2,1)}, bf16[1024,512]{1,0:T(8,128)(2,1)}, f32[2,32,1792]{2,1,0:T(8,128)}) custom-call(bf16[128,512]{1,0:T(8,128)(2,1)} %refs_0_.1, bf16[1024,512]{1,0:T(8,128)(2,1)} %refs_1_.1, s32[1,1024]{1,0:T(1,128)} %bitcast.6, s32[1,1024]{1,0:T(1,128)} %bitcast.7, s32[1,128]{1,0:T(1,128)} %refs_4_.1, ...), custom_call_target="tpu_custom_call" | custom-call | tf_op jit(solution)/shard_map/layer_backward/pallas_call | solution.py:531
  52.3 50.9 %results.1 = (bf16[128,512]{1,0:T(8,128)(2,1)}, bf16[1024,512]{1,0:T(8,128)(2,1)}, f32[32,1536]{1,0:T(8,128)}, f32[32,512]{1,0:T(8,128)}, f32[32,1024]{1,0:T(8,128)}, /*index=5*/f32[32,512]{1,0:T(8,128)}) custom-call(bf16[128,512]{1,0:T(8,128)(2,1)} %get-tuple-element.15.gnode_ref, bf16[1024,512]{1,0:T(8,128)(2,1)} %get-tuple-element.16.gedge_ref, ...), custom_call_target="tpu_custom_call" | custom-call | tf_op jit(solution)/shard_map/results/pallas_call | solution.py:559

commit v3 on v2

--- a/solution.py
+++ b/solution.py
@@ -9,6 +9,7 @@
 
 epsilon = 1e-05
 LANES = 128
+TILE = 32
 bf16 = jnp.bfloat16
 f32 = jnp.float32
 MESH = pl.DeviceIdType.MESH
@@ -184,11 +185,11 @@
 JOBS = ("node_first", "node_first", "node_second", "edge_second", "edge_first", "edge_first", "edge_first")
 
 
-def make_orders(bits):
+def make_phases(bits):
     upper = list(range(2, bits))
-    first = [0, 1] + upper
-    second = [1, 0] + upper
-    third = upper + [0, 1]
+    first = ([0], [1], upper)
+    second = ([1], [0], upper)
+    third = (upper, [0], [1])
     return (first, second, first, third, first, second, second)
 
 
@@ -198,10 +199,10 @@
     gnode_out, gedge_hbm, wsum_out = refs[11:14]
     (edge_ref, a_ref, b_ref, na_ref, nb_ref, gn_ref, ge_ref,
      ext, hot_s, hot_r, pre, act, normed, inv, cot, dout, dpre, dpre_t, updated, gedge,
-     halo_send, agg_send, agg_recv, agg, n_dpre, n_dout, n_act, spread, dnode,
+     halo_send, agg_send, agg_recv, agg, n_dpre, n_dout, n_act, n_pre, n_out, spread, dnode,
      back_send, back_recv, own_acc, own_send, own_recv, fin,
-     in_sem, out_sem, send_sem, recv_sem) = refs[14:53]
-    buffers = refs[53:]
+     in_sem, out_sem, send_sem, recv_sem) = refs[14:55]
+    buffers = refs[55:]
 
     patch = lax.axis_index("patch")
     core = lax.axis_index("shard")
@@ -219,10 +220,23 @@
     def bit_of(k):
         return lax.rem(lax.div(patch, jnp.int32(1 << k)), jnp.int32(2))
 
-    def across(k):
-        return patch + (1 - 2 * bit_of(k)) * (1 << k)
-
-    greet = [(patch, other), (nxt, core), (prv, core)] + [(across(k), core) for k in range(bits)]
+    def across(group, flips):
+        there = patch
+        for i, k in enumerate(group):
+            if (flips >> i) & 1:
+                there = there + (1 - 2 * bit_of(k)) * (1 << k)
+        return there
+
+    def part_of(group, flips):
+        place = 0
+        for i, k in enumerate(group):
+            bit = bit_of(k)
+            place = 2 * place + (1 - bit if (flips >> i) & 1 else bit)
+        return place
+
+    greet = [(patch, other), (nxt, core), (prv, core)]
+    for group in make_phases(bits)[0]:
+        greet += [(across(group, flips), core) for flips in range(1, 1 << len(group))]
     barrier = pltpu.get_barrier_semaphore()
     for target in greet:
         pl.semaphore_signal(barrier, inc=1, device_id=target, device_id_type=MESH)
@@ -266,9 +280,12 @@
     to_core_grad = send(gn_hbm, gn_ref.at[own_nodes], (patch, other))
 
     state = []
-    for k, order in enumerate(make_orders(bits)):
-        bufs = buffers[k * (2 + bits) : (k + 1) * (2 + bits)]
-        state.append(dict(order=order, bufs=bufs, copy=None, step=0, base=0, out=k * half))
+    for k, phases in enumerate(make_phases(bits)):
+        bufs = buffers[k * (2 + len(phases)) : (k + 1) * (2 + len(phases))]
+        order = [b for group in phases for b in group]
+        state.append(
+            dict(phases=phases, order=order, bufs=bufs, copies=[], step=0, base=0, left=patches, out=k * half)
+        )
 
     def gradient(k, left_t, right):
         job = state[k]
@@ -280,39 +297,56 @@
                 where = sum(((p >> b) & 1) << (bits - 1 - i) for i, b in enumerate(job["order"]))
                 block[side, where] = value[p * rows_out : (p + 1) * rows_out]
             if side is other:
-                job["copy"] = send(block.at[other], job["bufs"][1], (patch, other))
+                job["copies"] = [send(block.at[other], job["bufs"][1], (patch, other))]
 
     def advance(*ks):
         for k in ks:
             job = state[k]
-            step, base, block = job["step"], job["base"], job["bufs"][0]
-            if step > bits:
+            step, base, block, phases = job["step"], job["base"], job["bufs"][0], job["phases"]
+            if step > len(phases):
                 continue
-            got = job["bufs"][1 + step]
-            job["copy"].wait_recv()
-            if step == bits:
-                value = block[core, base].astype(f32) + got[0].astype(f32)
+            buf = job["bufs"][1 + step]
+            got = [buf] if step == 0 else [buf.at[i] for i in range(buf.shape[0])]
+            for copy in job["copies"]:
+                copy.wait_recv()
+            if step == len(phases):
+                value = block[core, base].astype(f32)
+                for part in got:
+                    value += part[0].astype(f32)
                 fin[core, :, job["out"] : job["out"] + half] = value
             else:
-                count = (patches >> step) // 2
-                bit = bit_of(job["order"][step])
-                away, stay = (1 - bit) * count, bit * count
+                group = phases[step]
+                count = job["left"] >> len(group)
 
                 def add(start):
                     where = pl.ds(base + start, count)
-                    block[core, where] = (
-                        block[core, where].astype(f32) + got[pl.ds(start, count)].astype(f32)
-                    ).astype(bf16)
-
-                add(away)
-                job["copy"] = send(
-                    block.at[core, pl.ds(base + away, count)],
-                    job["bufs"][2 + step],
-                    (across(job["order"][step]), core),
-                )
-                add(stay)
-                job["base"] = base + stay
+                    value = block[core, where].astype(f32)
+                    for part in got:
+                        value += part[pl.ds(start, count)].astype(f32)
+                    block[core, where] = value.astype(bf16)
+
+                job["copies"] = []
+                for flips in range(1, 1 << len(group)):
+                    start = part_of(group, flips) * count
+                    add(start)
+                    job["copies"].append(
+                        send(
+                            block.at[core, pl.ds(base + start, count)],
+                            job["bufs"][2 + step].at[flips - 1],
+                            (across(group, flips), core),
+                        )
+                    )
+                start = part_of(group, 0) * count
+                add(start)
+                job["base"], job["left"] = base + start, count
             job["step"] = step + 1
+
+    def tiles(rows, work):
+        def step(i, carry):
+            work(pl.ds(pl.multiple_of(i * TILE, TILE), TILE))
+            return carry
+
+        lax.fori_loop(0, rows // TILE, step, 0, unroll=4)
 
     hot_r[...] = lanes_hot(rcv_ref[...], own)
     loads["edge"].wait()
@@ -334,22 +368,30 @@
     to_next.wait_recv()
     for rows in chunks:
         taken = times(hot_s[rows, :], ext[...]).astype(bf16)
-        value = pre[rows, :] + times(taken, a_ref[width : 2 * width, :])
-        pre[rows, :] = value
-        hidden = (value * jax.nn.sigmoid(value)).astype(bf16)
-        act[rows, :] = hidden
-        scaled, scale = layer_norm(times(hidden, b_ref[...]))
+        pre[rows, :] += times(taken, a_ref[width : 2 * width, :])
+
+    def activate(rows):
+        value = pre[rows, :]
+        act[rows, :] = (value * jax.nn.sigmoid(value)).astype(bf16)
+
+    tiles(edges, activate)
+    for rows in chunks:
+        normed[rows, :] = times(act[rows, :], b_ref[...])
+
+    def normalize(rows):
+        scaled, scale = layer_norm(normed[rows, :])
         normed[rows, :] = scaled
         inv[rows, :] = scale
         updated[rows, :] = (edge_ref[rows, :].astype(f32) + scaled).astype(bf16)
+
+    tiles(edges, normalize)
     agg_send[...] = times(rows_hot(rcv_ref[...], own), updated[...]).astype(bf16)
     to_agg = send(agg_send, agg_recv, (patch, other))
 
-    @pl.loop(0, edges // LANES)
-    def _(i):
-        rows = pl.ds(pl.multiple_of(i * LANES, LANES), LANES)
+    def slope(rows):
         pre[rows, :] = swish_slope(pre[rows, :])
 
+    tiles(edges, slope)
     for name in ("na", "nb", "gn", "ge"):
         loads[name].wait()
     to_core_grad.wait_recv()
@@ -358,13 +400,23 @@
     node = ext[inner, :]
     aggregate = (agg_send[...].astype(f32) + agg_recv[...].astype(f32)).astype(bf16)
     agg[...] = aggregate
-    n_pre = times(node, na_ref[:width, :]) + times(aggregate, na_ref[width:, :])
-    hidden = (n_pre * jax.nn.sigmoid(n_pre)).astype(bf16)
-    n_act[...] = hidden
-    n_normed, n_inv = layer_norm(times(hidden, nb_ref[...]))
-    d_out = norm_backward(gn_ref[...].astype(f32), n_normed, n_inv)
-    n_dout[...] = d_out
-    d_pre = (times_transpose(d_out, nb_ref[...]) * swish_slope(n_pre)).astype(bf16)
+    n_pre[...] = times(node, na_ref[:width, :]) + times(aggregate, na_ref[width:, :])
+
+    def node_activate(rows):
+        value = n_pre[rows, :]
+        sig = jax.nn.sigmoid(value)
+        n_act[rows, :] = (value * sig).astype(bf16)
+        n_pre[rows, :] = sig * (1.0 + value * (1.0 - sig))
+
+    tiles(own, node_activate)
+    n_out[...] = times(n_act[...], nb_ref[...])
+
+    def node_norm(rows):
+        scaled, scale = layer_norm(n_out[rows, :])
+        n_dout[rows, :] = norm_backward(gn_ref[rows, :].astype(f32), scaled, scale)
+
+    tiles(own, node_norm)
+    d_pre = (times_transpose(n_dout[...], nb_ref[...]) * n_pre[...]).astype(bf16)
     n_dpre[...] = d_pre
     spread[...] = times_transpose(d_pre, na_ref[width:, :]).astype(bf16)
 
@@ -375,9 +427,14 @@
     gradient(2, n_dout[own_nodes, :].T, lambda lanes: n_act[own_nodes, lanes])
 
     for rows in chunks:
-        cotangent = ge_ref[rows, :].astype(f32) + times(hot_r[rows, :], spread[...])
+        cot[rows, :] = times(hot_r[rows, :], spread[...])
+
+    def edge_cotangent(rows):
+        cotangent = ge_ref[rows, :].astype(f32) + cot[rows, :]
         cot[rows, :] = cotangent
         dout[rows, :] = norm_backward(cotangent, normed[rows, :], inv[rows, :])
+
+    tiles(edges, edge_cotangent)
     advance(0, 1, 2)
     gradient(3, dout[...].T, lambda lanes: act[:, lanes])
     for rows in chunks:
@@ -425,7 +482,7 @@
     advance(5, 6, 0, 1, 2, 3, 4)
     to_own.wait_recv()
     gnode_out[...] = (own_acc[own_nodes, :] + own_recv[...].astype(f32) + dnode[...]).astype(bf16)
-    for _ in range(bits):
+    for _ in range(4):
         advance(0, 1, 2, 3, 4, 5, 6)
 
     send(fin.at[core], fin.at[core], (patch, other)).wait_recv()
@@ -478,12 +535,17 @@
     bits = patches.bit_length() - 1
     cfg = dict(patches=patches, rows_out=rows_out, half=half, chunk=chunk)
     job_bufs = []
-    for _ in JOBS:
+    copies = 9
+    for phases in make_phases(bits):
         shape = (rows_out, half)
         job_bufs.append(pltpu.VMEM((2, patches) + shape, bf16))
         job_bufs.append(pltpu.VMEM((patches,) + shape, bf16))
-        job_bufs += [pltpu.VMEM((patches >> (k + 1),) + shape, bf16) for k in range(bits)]
-    copies = 9 + len(JOBS) * (bits + 1)
+        left = patches
+        copies += 1
+        for group in phases:
+            left >>= len(group)
+            job_bufs.append(pltpu.VMEM(((1 << len(group)) - 1, left) + shape, bf16))
+            copies += (1 << len(group)) - 1
     scratch = [
         pltpu.VMEM(edge_latent.shape, bf16),
         pltpu.VMEM(w_edge_first.shape, bf16),
@@ -512,6 +574,8 @@
         pltpu.VMEM((own, units), bf16),
         pltpu.VMEM((own, width), bf16),
         pltpu.VMEM((own, units), bf16),
+        pltpu.VMEM((own, units), f32),
+        pltpu.VMEM((own, width), f32),
         pltpu.VMEM((own, width), bf16),
         pltpu.VMEM((node_rows, width), f32),
         pltpu.VMEM((halo2, width), bf16),
@@ -563,7 +627,7 @@
             jax.ShapeDtypeStruct((edges, width), bf16),
         ]
         + [jax.ShapeDtypeStruct((rows_out, m.shape[0]), f32) for m in matrices],
-        in_specs=[anywhere] * 3,
+        in_specs=[vmem] * 3,
         out_specs=[hbm] * 6,
         scratch_shapes=[pltpu.SemaphoreType.DMA((2 + 2 * len(JOBS),))],
         name="results",

time: 103 us -> 60.5 us (0.59)
  Pallas kernels: 102 us -> 59.6 us
    pallas_call x1, Pallas kernels: 50.9 us -> 2.66 us  [fused_body(): pl.pallas_call(functools.partial(finish_kernel, half), out_shape=[jax.Sha...]
    pallas_call x1, Pallas kernels: 51.6 us -> 57 us  [fused_body(): pl.pallas_call(functools.partial(fused_kernel, cfg), out_shape=[jax.Shape...]
where the time goes in v3:
time: 60.5 us; the launch traced here: 60.3 us
  Pallas kernels  59.6 us (99%)
  between operations  0.64 us (1%)
    pallas_call x1, Pallas kernels, fused_body(): pl.pallas_call(functools.partial(fused_kernel, cfg), out_shape=[jax.Shape...  57 us
    pallas_call x1, Pallas kernels, fused_body(): pl.pallas_call(functools.partial(finish_kernel, half), out_shape=[jax.Sha...  2.66 us

profile of v3, /device:TPU:1, one launch (start us, length us, event | category | flops | bytes accessed | tf_op | source)
XLA Modules:
  0.0 60.3 jit_solution(18328051156738987822)
XLA Ops:
  0.6 57.0 %layer_backward.1 = (bf16[128,512]{1,0:T(8,128)(2,1)}, bf16[1024,512]{1,0:T(8,128)(2,1)}, f32[2,32,1792]{2,1,0:T(8,128)}) custom-call(bf16[128,512]{1,0:T(8,128)(2,1)} %refs_0_.1, bf16[1024,512]{1,0:T(8,128)(2,1)} %refs_1_.1, s32[1,1024]{1,0:T(1,128)} %bitcast.6, s32[1,1024]{1,0:T(1,128)} %bitcast.7, s32[1,128]{1,0:T(1,128)} %refs_4_.1, ...), custom_call_target="tpu_custom_call" | custom-call | tf_op jit(solution)/shard_map/layer_backward/pallas_call | solution.py:595
  57.6 2.7 %results.1 = (bf16[128,512]{1,0:T(8,128)(2,1)}, bf16[1024,512]{1,0:T(8,128)(2,1)}, f32[32,1536]{1,0:T(8,128)}, f32[32,512]{1,0:T(8,128)}, f32[32,1024]{1,0:T(8,128)}, /*index=5*/f32[32,512]{1,0:T(8,128)}) custom-call(bf16[128,512]{1,0:T(8,128)(2,1)} %get-tuple-element.15.gnode_ref, bf16[1024,512]{1,0:T(8,128)(2,1)} %get-tuple-element.16.gedge_ref, ...), custom_call_target="tpu_custom_call" | custom-call | tf_op jit(solution)/shard_map/results/pallas_call | solution.py:623

commit v4 on v3

--- a/solution.py
+++ b/solution.py
@@ -199,10 +199,10 @@
     gnode_out, gedge_hbm, wsum_out = refs[11:14]
     (edge_ref, a_ref, b_ref, na_ref, nb_ref, gn_ref, ge_ref,
      ext, hot_s, hot_r, pre, act, normed, inv, cot, dout, dpre, dpre_t, updated, gedge,
-     halo_send, agg_send, agg_recv, agg, n_dpre, n_dout, n_act, n_pre, n_out, spread, dnode,
+     halo_send, agg_send, agg_recv, agg, n_dpre, n_dout, n_act, shares, spread, dnode,
      back_send, back_recv, own_acc, own_send, own_recv, fin,
-     in_sem, out_sem, send_sem, recv_sem) = refs[14:55]
-    buffers = refs[55:]
+     in_sem, out_sem, send_sem, recv_sem) = refs[14:54]
+    buffers = refs[54:]
 
     patch = lax.axis_index("patch")
     core = lax.axis_index("shard")
@@ -359,32 +359,23 @@
     to_prev = send(halo_send.at[pl.ds(0, halo)], ext.at[pl.ds(halo + own, halo)], (prv, core))
     to_next = send(halo_send.at[pl.ds(halo, halo)], ext.at[pl.ds(0, halo)], (nxt, core))
 
+    shares[:own, :] = times(ext[inner, :], a_ref[2 * width :, :]).astype(bf16)
     for rows in chunks:
-        taken = times(hot_r[rows, :], ext[inner, :]).astype(bf16)
-        pre[rows, :] += times(taken, a_ref[2 * width :, :])
+        pre[rows, :] += times(hot_r[rows, :], shares[:own, :])
     hot_s[...] = lanes_hot(snd_ref[...], total)
     loads["b"].wait()
     to_prev.wait_recv()
     to_next.wait_recv()
+    shares[...] = times(ext[...], a_ref[width : 2 * width, :]).astype(bf16)
     for rows in chunks:
-        taken = times(hot_s[rows, :], ext[...]).astype(bf16)
-        pre[rows, :] += times(taken, a_ref[width : 2 * width, :])
-
-    def activate(rows):
-        value = pre[rows, :]
-        act[rows, :] = (value * jax.nn.sigmoid(value)).astype(bf16)
-
-    tiles(edges, activate)
-    for rows in chunks:
-        normed[rows, :] = times(act[rows, :], b_ref[...])
-
-    def normalize(rows):
-        scaled, scale = layer_norm(normed[rows, :])
+        value = pre[rows, :] + times(hot_s[rows, :], shares[...])
+        pre[rows, :] = value
+        hidden = (value * jax.nn.sigmoid(value)).astype(bf16)
+        act[rows, :] = hidden
+        scaled, scale = layer_norm(times(hidden, b_ref[...]))
         normed[rows, :] = scaled
         inv[rows, :] = scale
         updated[rows, :] = (edge_ref[rows, :].astype(f32) + scaled).astype(bf16)
-
-    tiles(edges, normalize)
     agg_send[...] = times(rows_hot(rcv_ref[...], own), updated[...]).astype(bf16)
     to_agg = send(agg_send, agg_recv, (patch, other))
 
@@ -400,23 +391,13 @@
     node = ext[inner, :]
     aggregate = (agg_send[...].astype(f32) + agg_recv[...].astype(f32)).astype(bf16)
     agg[...] = aggregate
-    n_pre[...] = times(node, na_ref[:width, :]) + times(aggregate, na_ref[width:, :])
-
-    def node_activate(rows):
-        value = n_pre[rows, :]
-        sig = jax.nn.sigmoid(value)
-        n_act[rows, :] = (value * sig).astype(bf16)
-        n_pre[rows, :] = sig * (1.0 + value * (1.0 - sig))
-
-    tiles(own, node_activate)
-    n_out[...] = times(n_act[...], nb_ref[...])
-
-    def node_norm(rows):
-        scaled, scale = layer_norm(n_out[rows, :])
-        n_dout[rows, :] = norm_backward(gn_ref[rows, :].astype(f32), scaled, scale)
-
-    tiles(own, node_norm)
-    d_pre = (times_transpose(n_dout[...], nb_ref[...]) * n_pre[...]).astype(bf16)
+    n_pre = times(node, na_ref[:width, :]) + times(aggregate, na_ref[width:, :])
+    hidden = (n_pre * jax.nn.sigmoid(n_pre)).astype(bf16)
+    n_act[...] = hidden
+    n_normed, n_inv = layer_norm(times(hidden, nb_ref[...]))
+    d_out = norm_backward(gn_ref[...].astype(f32), n_normed, n_inv)
+    n_dout[...] = d_out
+    d_pre = (times_transpose(d_out, nb_ref[...]) * swish_slope(n_pre)).astype(bf16)
     n_dpre[...] = d_pre
     spread[...] = times_transpose(d_pre, na_ref[width:, :]).astype(bf16)
 
@@ -427,14 +408,9 @@
     gradient(2, n_dout[own_nodes, :].T, lambda lanes: n_act[own_nodes, lanes])
 
     for rows in chunks:
-        cot[rows, :] = times(hot_r[rows, :], spread[...])
-
-    def edge_cotangent(rows):
-        cotangent = ge_ref[rows, :].astype(f32) + cot[rows, :]
+        cotangent = ge_ref[rows, :].astype(f32) + times(hot_r[rows, :], spread[...])
         cot[rows, :] = cotangent
         dout[rows, :] = norm_backward(cotangent, normed[rows, :], inv[rows, :])
-
-    tiles(edges, edge_cotangent)
     advance(0, 1, 2)
     gradient(3, dout[...].T, lambda lanes: act[:, lanes])
     for rows in chunks:
@@ -574,8 +550,7 @@
         pltpu.VMEM((own, units), bf16),
         pltpu.VMEM((own, width), bf16),
         pltpu.VMEM((own, units), bf16),
-        pltpu.VMEM((own, units), f32),
-        pltpu.VMEM((own, width), f32),
+        pltpu.VMEM((total, units), bf16),
         pltpu.VMEM((own, width), bf16),
         pltpu.VMEM((node_rows, width), f32),
         pltpu.VMEM((halo2, width), bf16),

time: 60.5 us -> 53 us (0.88)
  Pallas kernels: 59.6 us -> 52.2 us
    pallas_call x1, Pallas kernels: 57 us -> 49.5 us  [fused_body(): pl.pallas_call(functools.partial(fused_kernel, cfg), out_shape=[jax.Shape...]
where the time goes in v4:
time: 53 us; the launch traced here: 52.8 us
  Pallas kernels  52.2 us (98%)
  between operations  0.64 us (1%)
    pallas_call x1, Pallas kernels, fused_body(): pl.pallas_call(functools.partial(fused_kernel, cfg), out_shape=[jax.Shape...  49.5 us
    pallas_call x1, Pallas kernels, fused_body(): pl.pallas_call(functools.partial(finish_kernel, half), out_shape=[jax.Sha...  2.66 us

profile of v4, /device:TPU:1, one launch (start us, length us, event | category | flops | bytes accessed | tf_op | source)
XLA Modules:
  0.0 52.8 jit_solution(1535553382804928194)
XLA Ops:
  0.6 49.5 %layer_backward.1 = (bf16[128,512]{1,0:T(8,128)(2,1)}, bf16[1024,512]{1,0:T(8,128)(2,1)}, f32[2,32,1792]{2,1,0:T(8,128)}) custom-call(bf16[128,512]{1,0:T(8,128)(2,1)} %refs_0_.1, bf16[1024,512]{1,0:T(8,128)(2,1)} %refs_1_.1, s32[1,1024]{1,0:T(1,128)} %bitcast.6, s32[1,1024]{1,0:T(1,128)} %bitcast.7, s32[1,128]{1,0:T(1,128)} %refs_4_.1, ...), custom_call_target="tpu_custom_call" | custom-call | tf_op jit(solution)/shard_map/layer_backward/pallas_call | solution.py:570
  50.1 2.7 %results.1 = (bf16[128,512]{1,0:T(8,128)(2,1)}, bf16[1024,512]{1,0:T(8,128)(2,1)}, f32[32,1536]{1,0:T(8,128)}, f32[32,512]{1,0:T(8,128)}, f32[32,1024]{1,0:T(8,128)}, /*index=5*/f32[32,512]{1,0:T(8,128)}) custom-call(bf16[128,512]{1,0:T(8,128)(2,1)} %get-tuple-element.15.gnode_ref, bf16[1024,512]{1,0:T(8,128)(2,1)} %get-tuple-element.16.gedge_ref, ...), custom_call_target="tpu_custom_call" | custom-call | tf_op jit(solution)/shard_map/results/pallas_call | solution.py:598
